TPU v7x, 512 devices: a whole 4x4x16 slice. The times are simulated.
512 devices in a mesh: dp: 16 (over x, z_hi), seq: 32 (over y, z_lo, core).
Axes of the slice: x: 4, y: 4, z: 16 (z_hi: 4, z_lo: 4; z = z_hi * 4 + z_lo), core: 2. Of those that a mesh axis runs over, the one named last changes fastest.
Arguments:
- queries: bfloat16 [16, 4096, 4096], P('dp', 'seq'), may hold values from -6 to 6
- products: bfloat16 [16, 4096, 4096], P('dp', 'seq'), may hold values from -6 to 6
- packed_grad: bfloat16 [16, 4096, 4096], P('dp', 'seq'), may hold values from -6 to 6
- packed_target: int32 [16, 4096], P('dp', 'seq'), may hold values from 0 to 4095, as said below
- short_filter: bfloat16 [3, 4096], replicated, may hold values from -3.5 to 3.5
- medium_filter: bfloat16 [128, 256], replicated, may hold values from -0.5 to 0.5
Outputs:
- input_grad: bfloat16 [16, 4096, 4096], P('dp', 'seq')
- medium_grad: float32 [128, 256], replicated
- short_grad: float32 [3, 4096], replicated
Inputs may be any that keep to these rules, and one draw needn't show every extreme that they name: `packed_target`: for each sequence a permutation of its positions. The 128 packed rows of one device hold at most 8 positions of any one device's 128 positions, and exactly 8 for some pairs of devices in every draw.
All inputs are finite; a program needn't handle non-finite values.
Results may differ from a plain program's by a relative error of at most 0.011.
Values may be sent and summed in bfloat16 or wider, within the bound.
No kernel may reach another device: no remote copies, remote signals or barrier semaphores. Data moves between devices by JAX's collectives and lax.ppermute only.
A program may use at most 128 MiB of HBM per device.

v0:
```python
import math

import jax
import jax.numpy as jnp
from jax import lax
from jax.sharding import PartitionSpec as P

highest = lax.Precision.HIGHEST


def shifted(value, axis, steps):
    count = lax.axis_size(axis)
    initial, last = (max(0, -steps), min(count, count - steps))
    return lax.ppermute(value, axis, [(source, source + steps) for source in range(initial, last)])


def dft_tables(size):
    half = size // 2
    times = jnp.arange(size, dtype=jnp.int32)
    freqs = jnp.arange(half + 1, dtype=jnp.int32)
    phase = (times[:, None] * freqs[None, :] % size).astype(jnp.float32) * (2.0 * math.pi / size)
    cosine = jnp.cos(phase)
    sine = jnp.sin(phase)[:, 1:half]
    forward = jnp.concatenate([cosine, -sine], axis=1).T
    weights = (
        jnp.concatenate(
            [
                jnp.ones((1,), jnp.float32),
                2.0 * jnp.ones((half - 1,), jnp.float32),
                jnp.ones((1,), jnp.float32),
            ]
        )
        / size
    )
    inverse = jnp.concatenate([cosine * weights[None, :], sine * (-2.0 / size)], axis=1)
    return (forward, inverse)


def spec_parts(spec, half):
    real_part = spec[: half + 1]
    zero_row = jnp.zeros((1,) + spec.shape[1:], spec.dtype)
    imag_part = jnp.concatenate([zero_row, spec[half + 1 :], zero_row], axis=0)
    return (real_part, imag_part)


def spec_times(left, right, half, conjugate):
    left_re, left_im = spec_parts(left, half)
    right_re, right_im = spec_parts(right, half)
    if conjugate:
        right_im = -right_im
    out_re = left_re * right_re - left_im * right_im
    out_im = left_re * right_im + left_im * right_re
    return jnp.concatenate([out_re, out_im[1:half]], axis=0)


def body(queries, products, packed_grad, packed_target, short_filter, medium_filter):
    row_count = queries.shape[1]
    channels = queries.shape[2]
    tap_count = medium_filter.shape[0]
    group_count = medium_filter.shape[1]
    per_group = channels // group_count
    short_count = short_filter.shape[0]
    reach = tap_count - 1
    short_reach = short_count - 1
    shards = lax.axis_size("seq")
    capacity = 2 * row_count // shards
    slot_count = shards * capacity
    size = row_count + tap_count
    half = size // 2
    forward, inverse = dft_tables(size)
    targets = packed_target[0]
    owner = targets // row_count
    local_pos = targets - owner * row_count
    owner_hot = (owner[:, None] == jnp.arange(shards)[None, :]).astype(jnp.int32)
    ranking = jnp.sum((jnp.cumsum(owner_hot, axis=0) - 1) * owner_hot, axis=1)
    slot_of = owner * capacity + ranking
    placing = slot_of[None, :] == jnp.arange(slot_count)[:, None]
    send_rows = jnp.dot(
        placing.astype(jnp.bfloat16), packed_grad[0], preferred_element_type=jnp.float32
    ).astype(jnp.bfloat16)
    send_pos = jnp.sum(jnp.where(placing, local_pos[None, :] + 1, 0), axis=1) - 1
    recv_rows, recv_pos = (
        lax.all_to_all(
            send_rows.reshape(shards, capacity, channels),
            "seq",
            split_axis=0,
            concat_axis=0,
            tiled=True,
        ),
        lax.all_to_all(
            send_pos.reshape(shards, capacity), "seq", split_axis=0, concat_axis=0, tiled=True
        ),
    )
    landing = (recv_pos.reshape(slot_count)[None, :] == jnp.arange(row_count)[:, None]).astype(
        jnp.bfloat16
    )
    routed = jnp.dot(
        landing, recv_rows.reshape(slot_count, channels), preferred_element_type=jnp.float32
    ).astype(jnp.bfloat16)
    query = queries[0]
    product = products[0]
    tail_rows = jnp.concatenate(
        [product[row_count - reach :], query[row_count - short_reach :]], axis=0
    )
    earlier = shifted(tail_rows, "seq", 1)
    query_ext = jnp.concatenate([earlier[reach:], query], axis=0)
    short_wide = short_filter.astype(jnp.float32)
    smoothed = sum(
        (
            short_wide[offset]
            * query_ext[short_reach - offset : short_reach - offset + row_count].astype(jnp.float32)
            for offset in range(short_count)
        )
    )
    filter_spec = jnp.dot(
        forward[:, :tap_count],
        medium_filter.astype(jnp.float32),
        precision=highest,
        preferred_element_type=jnp.float32,
    )
    filter_wide = jnp.repeat(filter_spec, per_group, axis=1)
    zero_one = jnp.zeros((1, channels), jnp.float32)
    product_ext = jnp.concatenate(
        [earlier[:reach].astype(jnp.float32), product.astype(jnp.float32), zero_one], axis=0
    )
    product_spec = jnp.dot(
        forward, product_ext, precision=highest, preferred_element_type=jnp.float32
    )
    hidden = jnp.dot(
        inverse[reach : reach + row_count],
        spec_times(product_spec, filter_wide, half, False),
        precision=highest,
        preferred_element_type=jnp.float32,
    )
    hidden_grad = (routed * smoothed).astype(jnp.bfloat16)
    smooth_grad = routed * hidden
    short_terms = jnp.stack(
        [
            jnp.sum(
                smooth_grad
                * query_ext[short_reach - offset : short_reach - offset + row_count].astype(
                    jnp.float32
                ),
                axis=0,
            )
            for offset in range(short_count)
        ]
    )
    placed = jnp.concatenate(
        [jnp.zeros((reach, channels), jnp.float32), hidden_grad.astype(jnp.float32), zero_one],
        axis=0,
    )
    grad_spec = jnp.dot(forward, placed, precision=highest, preferred_element_type=jnp.float32)
    cross = spec_times(grad_spec, product_spec, half, True)
    grouped = jnp.sum(cross.reshape(size, group_count, per_group), axis=2)
    medium_terms = jnp.dot(
        inverse[:tap_count], grouped, precision=highest, preferred_element_type=jnp.float32
    )
    spread = jnp.dot(
        inverse[: row_count + reach],
        spec_times(grad_spec, filter_wide, half, True),
        precision=highest,
        preferred_element_type=jnp.float32,
    )
    returned = shifted(spread[:reach], "seq", -1)
    gradient = spread[reach:] + jnp.concatenate(
        [jnp.zeros((row_count - reach, channels), jnp.float32), returned], axis=0
    )
    input_grad = gradient.astype(jnp.bfloat16)[None]
    short_total, medium_total = lax.psum((short_terms, medium_terms), ("dp", "seq"))
    positions_all = lax.axis_size("dp") * shards * row_count
    medium_grad = medium_total / math.sqrt(positions_all * per_group)
    short_grad = short_total / math.sqrt(positions_all)
    return (input_grad, medium_grad, short_grad)


def solution(mesh):
    in_specs = (
        P("dp", "seq", None),
        P("dp", "seq", None),
        P("dp", "seq", None),
        P("dp", "seq"),
        P(),
        P(),
    )
    out_specs = (P("dp", "seq", None), P(), P())
    return jax.shard_map(body, mesh=mesh, in_specs=in_specs, out_specs=out_specs, check_vma=False)
```

profile of v0, /device:TPU:1, one launch (start us, length us, event | category | flops | bytes accessed | tf_op | source)
XLA Modules:
  0.0 612.8 jit_solution(17364225218867093281)
XLA Ops:
  9.9 10.4 %all-to-all-start = ((s32[32,1,8]{2,1,0:T(1,128)}), s32[32,1,8]{2,1,0:T(1,128)S(1)}, u32[]{:S(2)}, u32[]{:S(2)}) async-start(s32[32,1,8]{2,1,0:T(1,128)} %bitcast.4), calls=%async_computation | async-start | bytes 32768 | tf_op jit(solution)/shard_map/all_to_all | solution.py:90
  22.3 5.2 all-to-all-done
  27.5 5.1 all-to-all-start.1
  35.0 3.5 collective-permute-start
  45.1 2.3 broadcast_in_dim.37
  47.4 3.6 copy.28
  52.7 2.4 broadcast_in_dim.38
  55.1 3.0 copy.30
  61.5 17.5 %collective-permute-done = bf16[129,4096]{1,0:T(8,128)(2,1)} collective-permute-done((bf16[129,4096]{1,0:T(8,128)(2,1)}, bf16[129,4096]{1,0:T(8,128)(2,1)}, u32[]{:S(2)}, u32[]{:S(2)}) %collective-permute-start) | collective-permute-done | bytes 1056800 | tf_op jit(solution)/shard_map/ppermute | solution.py:14
  80.5 4.1 fusion.3
  88.2 6.2 %all-to-all-done.1 = bf16[32,8,4096]{2,1,0:T(8,128)(2,1)} async-done(((bf16[32,8,4096]{2,1,0:T(8,128)(2,1)}), bf16[32,8,4096]{2,1,0:T(8,128)(2,1)}, u32[]{:S(2)}, u32[]{:S(2)}) %all-to-all-start.1) | async-done | bytes 2097184 | tf_op jit(solution)/shard_map/all_to_all | solution.py:83
  94.5 5.2 fusion.31
  99.7 4.0 fusion.2
  105.9 4.9 pad_maximum_fusion.6
  110.8 5.3 multiply_subtract_fusion
  117.5 5.4 fusion.24
  122.9 2.4 pad_maximum_fusion.4
  125.3 5.7 copy.32
  131.0 3.1 bitcast_reduce_fusion
  134.5 4.0 fusion.6
  144.4 6.9 %fusion.21 = (f32[4096]{0:T(1024)S(1)}, f32[4096]{0:T(1024)S(1)}, f32[4096]{0:T(1024)S(1)}) fusion(bf16[128,4096]{1,0:T(8,128)(2,1)} %bitcast.61, bf16[2,4096]{1,0:T(2,128)(2,1)S(1)} %slice.133, bf16[1,128,4096]{2,1,0:T(8,128)(2,1)} %param.6, f32[128,4096]{1,0:T(8,128)} %get-tuple-element.29, f32[127,4096]{1,0:T(8,128)} %get-tuple-element.13, ...), kind=kOutput, calls=%fused_computation.43 | convolution fusion | flops 1620070400 | bytes 8716288 | tf_op jit(solution)/shard_map/dot_general | solution.py:129
  151.3 115.1 %psum.15 = f32[3,4096]{1,0:T(4,128)S(1)} all-reduce(f32[3,4096]{1,0:T(4,128)S(1)} %pad_maximum_fusion.16), channel_id=1, replica_groups=mesh['dp'=16,'seq'=32] {'dp','seq'}, use_global_device_ids=true, to_apply=%region_8.9 | all-reduce | flops 12288 | bytes 98304 | tf_op jit(solution)/shard_map/psum | solution.py:170
  267.1 333.6 %all-reduce.3.cloned.1.call-done = f32[128,256]{1,0:T(8,128)} async-done(((f32[128,256]{1,0:T(8,128)}), f32[128,256]{1,0:T(8,128)}) %all-reduce.3.cloned.1.call-update) | async-done | bytes 131088 | tf_op jit(solution)/shard_map/psum | solution.py:170
  602.3 3.6 fusion.30
  (98 shorter events, 35.8 us)
Async XLA Ops:
  7.2 13.1 %copy-start = (bf16[1,128,4096]{2,1,0:T(8,128)(2,1)S(1)}, bf16[1,128,4096]{2,1,0:T(8,128)(2,1)}, u32[]{:S(2)}) copy-start(bf16[1,128,4096]{2,1,0:T(8,128)(2,1)} %param.8) | copy-start | bytes 3145732
  9.9 17.6 %all-to-all-start = ((s32[32,1,8]{2,1,0:T(1,128)}), s32[32,1,8]{2,1,0:T(1,128)S(1)}, u32[]{:S(2)}, u32[]{:S(2)}) async-start(s32[32,1,8]{2,1,0:T(1,128)} %bitcast.4), calls=%async_computation | async-start | bytes 32768 | tf_op jit(solution)/shard_map/all_to_all | solution.py:90
  22.3 11.2 %copy-start.14 = (bf16[1,128,4096]{2,1,0:T(8,128)(2,1)S(1)}, bf16[1,128,4096]{2,1,0:T(8,128)(2,1)}, u32[]{:S(2)}) copy-start(bf16[1,128,4096]{2,1,0:T(8,128)(2,1)} %param.7) | copy-start | bytes 3145732
  27.5 67.0 %all-to-all-start.1 = ((bf16[32,8,4096]{2,1,0:T(8,128)(2,1)}), bf16[32,8,4096]{2,1,0:T(8,128)(2,1)}, u32[]{:S(2)}, u32[]{:S(2)}) async-start(bf16[32,8,4096]{2,1,0:T(8,128)(2,1)} %fusion), calls=%async_computation.1 | async-start | bytes 4194304 | tf_op jit(solution)/shard_map/all_to_all | solution.py:83
  32.6 568.1 %all-reduce.3.cloned.1.call-start = ((), (), s32[]{:S(2)}) async-start(), calls=%async_computation.2 | async-start | bytes 262144 | tf_op jit(solution)/shard_map/psum | solution.py:170
  33.8 7.8 %copy-start.21 = (bf16[128,256]{1,0:T(8,128)(2,1)S(1)}, bf16[128,256]{1,0:T(8,128)(2,1)}, u32[]{:S(2)}) copy-start(bf16[128,256]{1,0:T(8,128)(2,1)} %param.11) | copy-start | bytes 196612
  33.8 8.1 %copy-start.20 = (bf16[3,4096]{1,0:T(4,128)(2,1)S(1)}, bf16[3,4096]{1,0:T(4,128)(2,1)}, u32[]{:S(2)}) copy-start(bf16[3,4096]{1,0:T(4,128)(2,1)} %param.10) | copy-start | bytes 73732
  33.8 8.8 %copy-start.26 = (f32[129]{0:T(256)S(1)}, f32[129]{0:T(256)}, u32[]{:S(2)}) copy-start(f32[129]{0:T(256)} %constant.50.clone.1) | copy-start | bytes 1552
  35.0 44.0 %collective-permute-start = (bf16[129,4096]{1,0:T(8,128)(2,1)}, bf16[129,4096]{1,0:T(8,128)(2,1)}, u32[]{:S(2)}, u32[]{:S(2)}) collective-permute-start(bf16[129,4096]{1,0:T(8,128)(2,1)} %pad_maximum_fusion.11), channel_id=1, source_target_pairs={{0,1},{1,2},{2,3},{3,4},{4,5},{5,6},{6,7},{7,8},{8,9},{9,10},{10,1... | collective-permute-start | bytes 3170312 | tf_op jit(solution)/shard_map/ppermute | solution.py:14
  60.2 20.3 %copy-start.18 = (f32[256,127]{1,0:T(8,128)S(1)}, f32[256,127]{1,0:T(8,128)}, u32[]{:S(2)}) copy-start(f32[256,127]{1,0:T(8,128)} %copy-done.17) | copy-start | bytes 390148
  61.5 19.0 %copy-start.12 = (f32[128,4096]{1,0:T(8,128)S(1)}, f32[128,4096]{1,0:T(8,128)}, u32[]{:S(2)}) copy-start(f32[128,4096]{1,0:T(8,128)} %bitcast_convert_fusion) | copy-start | bytes 6291460
  84.6 9.8 %copy-start.22 = (f32[1,4096]{1,0:T(1,128)S(1)}, f32[1,4096]{1,0:T(1,128)}, u32[]{:S(2)}) copy-start(f32[1,4096]{1,0:T(1,128)} %get-tuple-element.22) | copy-start | bytes 49156
  84.7 9.8 %copy-start.23 = (f32[1,4096]{1,0:T(1,128)S(1)}, f32[1,4096]{1,0:T(1,128)}, u32[]{:S(2)}) copy-start(f32[1,4096]{1,0:T(1,128)} %get-tuple-element.23) | copy-start | bytes 49156
  84.7 9.8 %copy-start.24 = (f32[1,4096]{1,0:T(1,128)S(1)}, f32[1,4096]{1,0:T(1,128)}, u32[]{:S(2)}) copy-start(f32[1,4096]{1,0:T(1,128)} %get-tuple-element.24) | copy-start | bytes 49156
  94.5 5.2 copy-start.25
  105.9 4.9 copy-start.5
  110.8 5.3 copy-start.8
  110.8 5.3 copy-start.9
  110.8 5.5 copy-start.10
  110.8 6.7 %copy-start.11 = (f32[129,4096]{1,0:T(8,128)S(1)}, f32[129,4096]{1,0:T(8,128)}, u32[]{:S(2)}) copy-start(f32[129,4096]{1,0:T(8,128)} %get-tuple-element.26) | copy-start | bytes 6340612
  125.3 8.8 %copy-start.15 = (f32[256,129]{1,0:T(8,128)S(1)}, f32[256,129]{1,0:T(8,128)}, u32[]{:S(2)}) copy-start(f32[256,129]{1,0:T(8,128)} %broadcast_multiply_fusion) | copy-start | bytes 396292
  138.5 5.8 copy-start.16
  141.4 461.0 %collective-permute-start.1 = (f32[127,4096]{1,0:T(8,128)}, f32[127,4096]{1,0:T(8,128)}, u32[]{:S(2)}, u32[]{:S(2)}) collective-permute-start(f32[127,4096]{1,0:T(8,128)} %slice.147), channel_id=1, source_target_pairs={{1,0},{2,1},{3,2},{4,3},{5,4},{6,5},{7,6},{8,7},{9,8},{10,9},{11,1... | collective-permute-start | bytes 6242312 | tf_op jit(solution)/shard_map/ppermute | solution.py:14
  600.7 5.3 copy-start.1
  (8 other events, 20.1 us)
Sparse Core Ops, SparseCore 0:
  144.5 456.1 all-reduce.2
where the time goes:
time: 613 us
  waiting for transfers between devices  363 us (59%)
  blocking collectives  115 us (19%)
  other arithmetic  37.9 us (6%)
  local copies, waits for them, and re-layouts  34.2 us (6%)
  matrix products  27.6 us (5%)
  starting transfers between devices  21 us (3%)
  between operations  14.4 us (2%)
    psum x1, waiting for transfers between devices, body(): lax.psum((short_terms, medium_terms), ('dp', 'seq'))  334 us
    psum x1, blocking collectives, body(): lax.psum((short_terms, medium_terms), ('dp', 'seq'))  115 us
    ppermute x2, waiting for transfers between devices, shifted(): lax.ppermute(value, axis, [(source, source + steps) for source in range(i...  17.5 us
  transfers between devices with their start and end apart: 5, of which 4 were waited for; matrix products, arithmetic and copies ran while one was open for 7% of the time, Pallas kernels for 0%

commit v1 on v0

v1 whole, which is shorter than its diff:
```python
import math

import jax
import jax.numpy as jnp
import numpy as np
from jax import lax
from jax.experimental import pallas as pl
from jax.experimental.pallas import tpu as pltpu
from jax.sharding import PartitionSpec as P

TILE = 512
LANES = 128
BLOCK_ROWS = 16
MIB = 1024 * 1024


def split(value):
    high = value.astype(jnp.bfloat16)
    low = (value - high.astype(jnp.float32)).astype(jnp.bfloat16)
    return high, low


def wave_table(rows):
    size = 2 * rows
    phase = (np.arange(size)[None, :] * (2 * np.arange(rows)[:, None] + 1)) % (2 * size)
    angle = phase * (math.pi / size)
    return np.concatenate([np.cos(angle), -np.sin(angle)], axis=0)


def halves(table):
    high = table.astype(jnp.bfloat16)
    low = (table - high.astype(np.float64)).astype(jnp.bfloat16)
    return jnp.asarray(high), jnp.asarray(low)


def mm(left, right):
    return jnp.dot(left, right, preferred_element_type=jnp.float32)


def forward(high, low, value):
    return mm(high, value) + mm(low, value)


def backward(high, low, value):
    top, rest = split(value)
    return mm(high, top) + (mm(low, top) + mm(high, rest))


def halved(spec):
    half = spec.shape[0] // 2
    return spec[:half], spec[half:]


def filter_spec(taps, high, low, per_group):
    tap_count, group_count = taps.shape
    channel = lax.broadcasted_iota(jnp.int32, (group_count, TILE), 1) + pl.program_id(0) * TILE
    group = lax.broadcasted_iota(jnp.int32, (group_count, TILE), 0)
    first = group * per_group
    expand = ((channel >= first) & (channel < first + per_group)).astype(jnp.bfloat16)
    wide = mm(taps, expand).astype(jnp.bfloat16)
    return forward(high[:, :tap_count], low[:, :tap_count], wide)


def delayed(query, tail, steps):
    moved = pltpu.roll(query, steps, 0)
    row = lax.broadcasted_iota(jnp.int32, query.shape, 0)
    for index in range(steps):
        source = tail.shape[0] - steps + index
        moved = jnp.where(row == index, tail[source : source + 1], moved)
    return moved


def pack_kernel(capacity, target_ref, grad_ref, out_ref):
    rows, channels = grad_ref.shape
    slots = out_ref.shape[0]
    wide = jnp.broadcast_to(target_ref[...].astype(jnp.float32), (rows, rows))
    across = wide.astype(jnp.int32)
    down = wide.T.astype(jnp.int32)
    upper = lax.broadcasted_iota(jnp.int32, (rows, rows), 0)
    right = lax.broadcasted_iota(jnp.int32, (rows, rows), 1)
    owner = lax.div(across, rows)
    earlier = (owner == lax.div(down, rows)) & (upper < right)
    rank = jnp.sum(earlier.astype(jnp.float32), axis=0, keepdims=True).astype(jnp.int32)
    slot = owner[:1] * capacity + rank
    placing = (lax.broadcasted_iota(jnp.int32, (slots, rows), 0) == slot).astype(jnp.bfloat16)
    landing = (lax.rem(down, rows) == right).astype(jnp.bfloat16)
    for start in range(0, channels, TILE):
        out_ref[:, start : start + TILE] = mm(placing, grad_ref[:, start : start + TILE]).astype(
            jnp.bfloat16
        )
    out_ref[:, channels:] = mm(placing, landing).astype(jnp.bfloat16)


def early_kernel(
    per_group,
    query_ref,
    tail_ref,
    own_ref,
    prev_ref,
    short_ref,
    taps_ref,
    fh_ref,
    fl_ref,
    ih_ref,
    il_ref,
    smooth_ref,
    hidden_ref,
    spec_ref,
):
    rows = own_ref.shape[0]
    spec = forward(
        fh_ref[...], fl_ref[...], jnp.concatenate([prev_ref[...], own_ref[...]], axis=0)
    )
    spec_ref[...] = spec
    wave = filter_spec(taps_ref[...], fh_ref, fl_ref, per_group)
    sr, si = halved(spec)
    wr, wi = halved(wave)
    product = jnp.concatenate([sr * wr - si * wi, sr * wi + si * wr], axis=0)
    hidden_ref[...] = backward(ih_ref[rows:], il_ref[rows:], product)
    query = query_ref[...].astype(jnp.float32)
    tail = tail_ref[...].astype(jnp.float32)
    short = short_ref[...].astype(jnp.float32)
    total = short[0:1] * query
    for offset in range(1, short.shape[0]):
        total = total + short[offset : offset + 1] * delayed(query, tail, offset)
    smooth_ref[...] = total


def grad_kernel(
    per_group,
    short_count,
    land_ref,
    recv_ref,
    smooth_ref,
    hidden_ref,
    spec_ref,
    query_ref,
    tail_ref,
    fh_ref,
    fl_ref,
    ch_ref,
    cl_ref,
    hgrad_ref,
    sums_ref,
):
    rows = hgrad_ref.shape[0]
    groups = TILE // per_group
    routed = lax.dot_general(
        land_ref[...],
        recv_ref[...],
        (((0,), (0,)), ((), ())),
        preferred_element_type=jnp.float32,
    )
    hgrad = (routed * smooth_ref[...]).astype(jnp.bfloat16)
    hgrad_ref[...] = hgrad
    sgrad = routed * hidden_ref[...]
    query = query_ref[...].astype(jnp.float32)
    tail = tail_ref[...].astype(jnp.float32)
    terms = [jnp.sum(sgrad * query, axis=0, keepdims=True)]
    for offset in range(1, short_count):
        terms.append(jnp.sum(sgrad * delayed(query, tail, offset), axis=0, keepdims=True))
    terms.append(jnp.zeros((8 - short_count, TILE), jnp.float32))
    short_terms = jnp.concatenate(terms, axis=0)
    gr, gi = halved(forward(fh_ref[:, rows:], fl_ref[:, rows:], hgrad))
    pr, pi = halved(spec_ref[...])
    cross = jnp.concatenate([gr * pr + gi * pi, gi * pr - gr * pi], axis=0)
    first = lax.broadcasted_iota(jnp.int32, (groups, TILE), 0) * per_group
    channel = lax.broadcasted_iota(jnp.int32, (groups, TILE), 1)
    member = ((channel >= first) & (channel < first + per_group)).astype(jnp.bfloat16)
    dims = (((1,), (1,)), ((), ()))
    top, rest = split(cross)
    grouped = lax.dot_general(member, top, dims, preferred_element_type=jnp.float32)
    grouped += lax.dot_general(member, rest, dims, preferred_element_type=jnp.float32)
    top, rest = split(grouped)
    lagged = mm(top, ch_ref[...]) + (mm(top, cl_ref[...]) + mm(rest, ch_ref[...]))
    for part in range(TILE // LANES):
        sums_ref[part, :8] = lagged[8 * part : 8 * part + 8]
        sums_ref[part, 8:] = short_terms[:, part * LANES : (part + 1) * LANES]


def input_kernel(
    per_group, own_ref, next_ref, taps_ref, fh_ref, fl_ref, ih_ref, il_ref, out_ref
):
    rows = own_ref.shape[0]
    spec = forward(
        fh_ref[...], fl_ref[...], jnp.concatenate([own_ref[...], next_ref[...]], axis=0)
    )
    wave = filter_spec(taps_ref[...], fh_ref, fl_ref, per_group)
    gr, gi = halved(spec)
    wr, wi = halved(wave)
    product = jnp.concatenate([gr * wr + gi * wi, gi * wr - gr * wi], axis=0)
    out_ref[...] = backward(ih_ref[:rows], il_ref[:rows], product).astype(jnp.bfloat16)


def last_kernel(medium_scale, short_scale, sums_ref, medium_ref, short_ref):
    parts = sums_ref.shape[0]
    groups = medium_ref.shape[1]
    medium = sums_ref[:, :8, :].reshape(groups, LANES)
    medium_ref[...] = medium.T * medium_scale
    for part in range(parts):
        short_ref[:, part * LANES : (part + 1) * LANES] = (
            sums_ref[part, 8 : 8 + short_ref.shape[0]] * short_scale
        )


def params(mib):
    return pltpu.CompilerParams(vmem_limit_bytes=mib * MIB)


def cost(flops, moved):
    return pl.CostEstimate(flops=flops, bytes_accessed=moved, transcendentals=0)


def columns(rows):
    return pl.BlockSpec((rows, TILE), lambda step: (0, step))


def whole(array):
    return pl.BlockSpec(array.shape, lambda step: (0,) * array.ndim)


def body(queries, products, packed_grad, packed_target, short_filter, medium_filter):
    query, product = queries[0], products[0]
    rows, channels = product.shape
    group_count = medium_filter.shape[1]
    per_group = channels // group_count
    short_count = short_filter.shape[0]
    shards, copies = lax.axis_size("seq"), lax.axis_size("dp")
    capacity = 2 * rows // shards
    slots = shards * capacity
    width = channels + rows
    steps = channels // TILE
    table = wave_table(rows)
    fh, fl = halves(table)
    ih, il = halves(table.T / rows)
    ch, cl = halves(table[:, :rows] / rows)
    f32, bf16 = jnp.float32, jnp.bfloat16

    with jax.named_scope("pack"):
        send = pl.pallas_call(
            lambda *refs: pack_kernel(capacity, *refs),
            out_shape=jax.ShapeDtypeStruct((slots, width), bf16),
            compiler_params=params(24),
            cost_estimate=cost(2 * slots * rows * width, 8 * MIB // 2),
        )(packed_target, packed_grad[0])
    with jax.named_scope("route"):
        recv = lax.all_to_all(
            send.reshape(shards, capacity, width), "seq", split_axis=0, concat_axis=0, tiled=True
        ).reshape(slots, width)
    with jax.named_scope("halo"):
        onward = [(index, index + 1) for index in range(shards - 1)]
        prev = lax.ppermute(product, "seq", onward)
        tail = lax.ppermute(query[rows - 16 :], "seq", onward)
    with jax.named_scope("early"):
        smoothed, hidden, spec = pl.pallas_call(
            lambda *refs: early_kernel(per_group, *refs),
            grid=(steps,),
            in_specs=[
                columns(rows),
                columns(16),
                columns(rows),
                columns(rows),
                columns(short_count),
                whole(medium_filter),
                whole(fh),
                whole(fl),
                whole(ih),
                whole(il),
            ],
            out_specs=[columns(rows), columns(rows), columns(2 * rows)],
            out_shape=[
                jax.ShapeDtypeStruct((rows, channels), f32),
                jax.ShapeDtypeStruct((rows, channels), f32),
                jax.ShapeDtypeStruct((2 * rows, channels), f32),
            ],
            compiler_params=params(32),
            cost_estimate=cost(16 * rows * 2 * rows * channels, 12 * MIB),
        )(query, tail, product, prev, short_filter, medium_filter, fh, fl, ih, il)
    with jax.named_scope("grads"):
        hgrad, sums = pl.pallas_call(
            lambda *refs: grad_kernel(per_group, short_count, *refs),
            grid=(steps,),
            in_specs=[
                pl.BlockSpec((slots, rows), lambda step: (0, channels // rows)),
                columns(slots),
                columns(rows),
                columns(rows),
                columns(2 * rows),
                columns(rows),
                columns(16),
                whole(fh),
                whole(fl),
                whole(ch),
                whole(cl),
            ],
            out_specs=[
                columns(rows),
                pl.BlockSpec((TILE // LANES, BLOCK_ROWS, LANES), lambda step: (step, 0, 0)),
            ],
            out_shape=[
                jax.ShapeDtypeStruct((rows, channels), bf16),
                jax.ShapeDtypeStruct((channels // LANES, BLOCK_ROWS, LANES), f32),
            ],
            compiler_params=params(32),
            cost_estimate=cost(10 * rows * 2 * rows * channels, 12 * MIB),
        )(recv, recv, smoothed, hidden, spec, query, tail, fh, fl, ch, cl)
    with jax.named_scope("sums_seq"):
        mine = jnp.sum(lax.all_to_all(sums, "seq", 0, 0, tiled=True), axis=0)
    with jax.named_scope("sums_dp"):
        spread = jnp.broadcast_to(mine[None], (copies, BLOCK_ROWS, LANES))
        mine = jnp.sum(lax.all_to_all(spread, "dp", 0, 0, tiled=True), axis=0)
    with jax.named_scope("sums_all"):
        spread = jnp.broadcast_to(mine[None], (shards, BLOCK_ROWS, LANES))
        total = lax.all_to_all(spread, "seq", 0, 0, tiled=True)
    with jax.named_scope("later"):
        following = lax.ppermute(
            hgrad, "seq", [(index + 1, index) for index in range(shards - 1)]
        )
    with jax.named_scope("input_grad"):
        input_grad = pl.pallas_call(
            lambda *refs: input_kernel(per_group, *refs),
            grid=(steps,),
            in_specs=[columns(rows), columns(rows)]
            + [whole(medium_filter), whole(fh), whole(fl), whole(ih), whole(il)],
            out_specs=columns(rows),
            out_shape=jax.ShapeDtypeStruct((rows, channels), bf16),
            compiler_params=params(32),
            cost_estimate=cost(16 * rows * 2 * rows * channels, 4 * MIB),
        )(hgrad, following, medium_filter, fh, fl, ih, il)
    with jax.named_scope("finish"):
        positions = copies * shards * rows
        medium_scale = 1.0 / math.sqrt(positions * per_group)
        short_scale = 1.0 / math.sqrt(positions)
        medium_grad, short_grad = pl.pallas_call(
            lambda *refs: last_kernel(medium_scale, short_scale, *refs),
            out_shape=[
                jax.ShapeDtypeStruct((rows, group_count), f32),
                jax.ShapeDtypeStruct((short_count, channels), f32),
            ],
        )(total)
    return input_grad[None], medium_grad, short_grad


def solution(mesh):
    in_specs = (
        P("dp", "seq", None),
        P("dp", "seq", None),
        P("dp", "seq", None),
        P("dp", "seq"),
        P(),
        P(),
    )
    out_specs = (P("dp", "seq", None), P(), P())
    return jax.shard_map(body, mesh=mesh, in_specs=in_specs, out_specs=out_specs, check_vma=False)
```

time: 613 us -> 192 us (0.31)
  the two profiles are of different devices: /device:TPU:1 before, /device:TPU:11 now
where the time goes in v1:
time: 192 us; the launch traced here: 191 us
  waiting for transfers between devices  54.5 us (28%)
  starting transfers between devices  50.1 us (26%)
  Pallas kernels  29.3 us (15%)
  blocking collectives  29.3 us (15%)
  local copies, waits for them, and re-layouts  27.3 us (14%)
    ppermute x1, waiting for transfers between devices, body(): tail = lax.ppermute(query[rows - 16:], 'seq', onward)  42.8 us
    all_to_all x1, blocking collectives, body(): mine = jnp.sum(lax.all_to_all(sums, 'seq', 0, 0, tiled=True), axis=0)  29.3 us
    unnamed x54, local copies, waits for them, and re-layouts  25.9 us
    all_to_all x1, starting transfers between devices, body(): total = lax.all_to_all(spread, 'seq', 0, 0, tiled=True)  18.4 us
    all_to_all x1, starting transfers between devices, body(): mine = jnp.sum(lax.all_to_all(spread, 'dp', 0, 0, tiled=True), axis=0)  14.8 us
    all_to_all x1, waiting for transfers between devices, body(): mine = jnp.sum(lax.all_to_all(spread, 'dp', 0, 0, tiled=True), axis=0)  11.7 us
    pallas_call x1, Pallas kernels, body(): pl.pallas_call(lambda *refs: grad_kernel(per_group, short_count, *refs),...  9.66 us
    all_to_all x1, starting transfers between devices, body(): lax.all_to_all(send.reshape(shards, capacity, width), 'seq', split_axis=0...  9.59 us
  transfers between devices with their start and end apart: 6, of which 2 were waited for; matrix products, arithmetic and copies ran while one was open for 0% of the time, Pallas kernels for 9%

profile of v1, /device:TPU:11, one launch (start us, length us, event | category | flops | bytes accessed | tf_op | source)
XLA Modules:
  0.0 191.3 jit_solution(862580275423036745)
XLA Ops:
  0.6 1.2 copy-done.8
  3.3 1.4 copy-done
  4.7 9.6 %all-to-all-start = ((bf16[32,8,4224]{2,1,0:T(8,128)(2,1)}), bf16[32,8,4224]{2,1,0:T(8,128)(2,1)S(1)}, u32[]{:S(2)}, u32[]{:S(2)}) async-start(bf16[32,8,4224]{2,1,0:T(8,128)(2,1)} %bitcast.10), calls=%async_computation | async-start | bytes 4325376 | tf_op jit(solution)/shard_map/route/all_to_all | solution.py:247
  14.3 3.3 %collective-permute-start.1 = (bf16[128,4096]{1,0:T(8,128)(2,1)}, bf16[128,4096]{1,0:T(8,128)(2,1)S(1)}, u32[]{:S(2)}, u32[]{:S(2)}) collective-permute-start(bf16[128,4096]{1,0:T(8,128)(2,1)} %bitcast.14), channel_id=1, source_target_pairs={{0,1},{1,2},{2,3},{3,4},{4,5},{5,6},{6,7},{7,8},{8,9},{9,10},{10,1... | collective-permute-start | bytes 3145736 | tf_op jit(solution)/shard_map/halo/ppermute | solution.py:252
  17.7 2.1 %collective-permute-start = (bf16[16,4096]{1,0:T(8,128)(2,1)S(1)}, bf16[16,4096]{1,0:T(8,128)(2,1)S(1)}, u32[]{:S(2)}, u32[]{:S(2)}) collective-permute-start(bf16[16,4096]{1,0:T(8,128)(2,1)S(1)} %slice_bitcast_fusion), channel_id=1, source_target_pairs={{0,1},{1,2},{2,3},{3,4},{4,5},{5,6},{6,7},{7,8},{8,9},{9,10},{10,1... | collective-permute-start | bytes 393224 | tf_op jit(solution)/shard_map/halo/ppermute | solution.py:253
  19.8 42.8 %collective-permute-done.refs_1_.refs_6_ = bf16[16,4096]{1,0:T(8,128)(2,1)S(1)} collective-permute-done((bf16[16,4096]{1,0:T(8,128)(2,1)S(1)}, bf16[16,4096]{1,0:T(8,128)(2,1)S(1)}, u32[]{:S(2)}, u32[]{:S(2)}) %collective-permute-start) | collective-permute-done | bytes 131104 | tf_op jit(solution)/shard_map/halo/ppermute | solution.py:253
  62.6 1.2 copy-done.16
  67.2 8.8 %early.1 = (f32[128,4096]{1,0:T(8,128)S(1)}, f32[128,4096]{1,0:T(8,128)S(1)}, f32[256,4096]{1,0:T(8,128)S(1)}) custom-call(bf16[128,4096]{1,0:T(8,128)(2,1)S(1)} %bitcast.11, bf16[16,4096]{1,0:T(8,128)(2,1)S(1)} %collective-permute-done.refs_1_.refs_6_, bf16[128,4096]{1,0:T(8,128)(2,1)S(1)} %bitcast.15, ...), custom_call_target="tpu_custom_call" | custom-call | flops 2147483648 | bytes 12582912 | tf_op jit(solution)/shard_map/early/pallas_call | solution.py:255
  76.0 1.9 %copy-done.1 = f32[256,4096]{1,0:T(8,128)} copy-done((f32[256,4096]{1,0:T(8,128)}, f32[256,4096]{1,0:T(8,128)S(1)}, u32[]{:S(2)}) %copy-start.1) | copy-done | bytes 4194328
  78.0 1.4 copy-done.3
  79.4 1.4 copy-done.5
  81.4 2.2 %copy-done.2 = f32[256,4096]{1,0:T(8,128)S(1)} copy-done((f32[256,4096]{1,0:T(8,128)S(1)}, f32[256,4096]{1,0:T(8,128)}, u32[]{:S(2)}) %copy-start.2) | copy-done | bytes 4194328
  83.6 1.6 copy-done.4
  85.2 1.6 copy-done.6
  88.5 9.7 %grads.1 = (bf16[128,4096]{1,0:T(8,128)(2,1)S(1)}, f32[32,16,128]{2,1,0:T(8,128)S(1)}) custom-call(bf16[256,4224]{1,0:T(8,128)(2,1)S(1)} %bitcast.8, bf16[256,4224]{1,0:T(8,128)(2,1)S(1)} %bitcast.9, f32[128,4096]{1,0:T(8,128)S(1)} %copy-done.4, f32[128,4096]{1,0:T(8,128)S(1)} %copy-done.6, f32[256,4096]{1,0:T(8,128)S(1)} %copy-done.2, ...), custom_call_target="tpu_custom_call" | custom-call | flops 1342177280 | bytes 12582912 | tf_op jit(solution)/shard_map/grads/pallas_call | solution.py:280
  98.2 1.0 copy-done.17
  99.2 29.3 %all_to_all.20 = f32[32,16,128]{2,1,0:T(8,128)S(1)} all-to-all(f32[32,16,128]{2,1,0:T(8,128)S(1)} %get-tuple-element.14), channel_id=1, replica_groups=mesh['dp'=16,'seq'=32] {'seq'}, dimensions={0} | all-to-all | bytes 524288 | tf_op jit(solution)/shard_map/sums_seq/all_to_all | solution.py:308
  129.1 14.8 %all-to-all-start.2 = ((f32[16,16,128]{2,1,0:T(8,128)}), f32[16,16,128]{2,1,0:T(8,128)S(1)}, u32[]{:S(2)}, u32[]{:S(2)}) async-start(f32[16,16,128]{2,1,0:T(8,128)} %broadcast_in_dim.7), calls=%async_computation.2 | async-start | bytes 262144 | tf_op jit(solution)/shard_map/sums_dp/all_to_all | solution.py:311
  144.0 1.9 collective-permute-start.2
  145.9 11.7 %all-to-all-done.2 = f32[16,16,128]{2,1,0:T(8,128)S(1)} async-done(((f32[16,16,128]{2,1,0:T(8,128)}), f32[16,16,128]{2,1,0:T(8,128)S(1)}, u32[]{:S(2)}, u32[]{:S(2)}) %all-to-all-start.2) | async-done | bytes 131104 | tf_op jit(solution)/shard_map/sums_dp/all_to_all | solution.py:311
  158.3 18.4 %all-to-all-start.3 = ((f32[32,16,128]{2,1,0:T(8,128)}), f32[32,16,128]{2,1,0:T(8,128)S(1)}, u32[]{:S(2)}, u32[]{:S(2)}) async-start(f32[32,16,128]{2,1,0:T(8,128)} %broadcast_in_dim.8), calls=%async_computation.3 | async-start | bytes 524288 | tf_op jit(solution)/shard_map/sums_all/all_to_all | solution.py:314
  176.7 1.2 copy-done.18
  180.6 8.3 %input_grad.1 = bf16[128,4096]{1,0:T(8,128)(2,1)} custom-call(bf16[128,4096]{1,0:T(8,128)(2,1)S(1)} %copy-done.18, bf16[128,4096]{1,0:T(8,128)(2,1)S(1)} %collective-permute-done.2.refs_1_, bf16[128,256]{1,0:T(8,128)(2,1)S(1)} %copy-done.20, bf16[256,256]{1,0:T(8,128)(2,1)S(1)} %copy-done.10, bf16[256,256]{1,0:T(8,128)(2,1)S(1)} %copy-done.9, ...), custom_call_target="tpu_custom_call" | custom-call | flops 2147483648 | bytes 4194304 | tf_op jit(solution)/shard_map/input_grad/pallas_call | solution.py:320
  189.6 1.7 finish.1
  (53 shorter events, 12.1 us)
Async XLA Ops:
  0.6 1.2 copy-start.8
  3.3 1.4 copy-start
  4.7 13.0 %copy-start.7 = (bf16[1,128,4096]{2,1,0:T(8,128)(2,1)S(1)}, bf16[1,128,4096]{2,1,0:T(8,128)(2,1)}, u32[]{:S(2)}) copy-start(bf16[1,128,4096]{2,1,0:T(8,128)(2,1)} %param.12) | copy-start | bytes 3145732
  4.7 57.8 %copy-start.9 = (bf16[256,256]{1,0:T(8,128)(2,1)S(1)}, bf16[256,256]{1,0:T(8,128)(2,1)}, u32[]{:S(2)}) copy-start(bf16[256,256]{1,0:T(8,128)(2,1)} %constant.15.clone.refs_7_.refs_8_.refs_4_) | copy-start | bytes 393220
  4.7 57.8 %copy-start.10 = (bf16[256,256]{1,0:T(8,128)(2,1)S(1)}, bf16[256,256]{1,0:T(8,128)(2,1)}, u32[]{:S(2)}) copy-start(bf16[256,256]{1,0:T(8,128)(2,1)} %constant.14.clone.refs_6_.refs_7_.refs_3_) | copy-start | bytes 393220
  4.7 76.7 %all-to-all-start = ((bf16[32,8,4224]{2,1,0:T(8,128)(2,1)}), bf16[32,8,4224]{2,1,0:T(8,128)(2,1)S(1)}, u32[]{:S(2)}, u32[]{:S(2)}) async-start(bf16[32,8,4224]{2,1,0:T(8,128)(2,1)} %bitcast.10), calls=%async_computation | async-start | bytes 4325376 | tf_op jit(solution)/shard_map/route/all_to_all | solution.py:247
  14.3 48.2 %collective-permute-start.1 = (bf16[128,4096]{1,0:T(8,128)(2,1)}, bf16[128,4096]{1,0:T(8,128)(2,1)S(1)}, u32[]{:S(2)}, u32[]{:S(2)}) collective-permute-start(bf16[128,4096]{1,0:T(8,128)(2,1)} %bitcast.14), channel_id=1, source_target_pairs={{0,1},{1,2},{2,3},{3,4},{4,5},{5,6},{6,7},{7,8},{8,9},{9,10},{10,1... | collective-permute-start | bytes 3145736 | tf_op jit(solution)/shard_map/halo/ppermute | solution.py:252
  17.7 44.8 %collective-permute-start = (bf16[16,4096]{1,0:T(8,128)(2,1)S(1)}, bf16[16,4096]{1,0:T(8,128)(2,1)S(1)}, u32[]{:S(2)}, u32[]{:S(2)}) collective-permute-start(bf16[16,4096]{1,0:T(8,128)(2,1)S(1)} %slice_bitcast_fusion), channel_id=1, source_target_pairs={{0,1},{1,2},{2,3},{3,4},{4,5},{5,6},{6,7},{7,8},{8,9},{9,10},{10,1... | collective-permute-start | bytes 393224 | tf_op jit(solution)/shard_map/halo/ppermute | solution.py:253
  62.6 1.2 copy-start.16
  65.4 0.9 copy-start.22
  66.3 0.9 copy-start.24
  67.2 14.2 %copy-start.13 = (bf16[256,128]{1,0:T(8,128)(2,1)S(1)}, bf16[256,128]{1,0:T(8,128)(2,1)}, u32[]{:S(2)}) copy-start(bf16[256,128]{1,0:T(8,128)(2,1)} %constant.19.clone.refs_10_) | copy-start | bytes 196612
  76.0 2.0 %copy-start.1 = (f32[256,4096]{1,0:T(8,128)}, f32[256,4096]{1,0:T(8,128)S(1)}, u32[]{:S(2)}) copy-start(f32[256,4096]{1,0:T(8,128)S(1)} %get-tuple-element.12.refs_4_) | copy-start | bytes 12582916
  78.0 1.4 copy-start.3
  79.4 1.4 copy-start.5
  81.4 2.2 %copy-start.2 = (f32[256,4096]{1,0:T(8,128)S(1)}, f32[256,4096]{1,0:T(8,128)}, u32[]{:S(2)}) copy-start(f32[256,4096]{1,0:T(8,128)} %copy-done.1) | copy-start | bytes 12582916
  83.6 1.6 copy-start.4
  85.2 1.6 copy-start.6
  98.2 1.0 copy-start.17
  129.1 28.5 %all-to-all-start.2 = ((f32[16,16,128]{2,1,0:T(8,128)}), f32[16,16,128]{2,1,0:T(8,128)S(1)}, u32[]{:S(2)}, u32[]{:S(2)}) async-start(f32[16,16,128]{2,1,0:T(8,128)} %broadcast_in_dim.7), calls=%async_computation.2 | async-start | bytes 262144 | tf_op jit(solution)/shard_map/sums_dp/all_to_all | solution.py:311
  144.0 32.7 %collective-permute-start.2 = (bf16[128,4096]{1,0:T(8,128)(2,1)}, bf16[128,4096]{1,0:T(8,128)(2,1)S(1)}, u32[]{:S(2)}, u32[]{:S(2)}) collective-permute-start(bf16[128,4096]{1,0:T(8,128)(2,1)} %copy-done.17), channel_id=1, source_target_pairs={{1,0},{2,1},{3,2},{4,3},{5,4},{6,5},{7,6},{8,7},{9,8},{10,9},{11,1... | collective-permute-start | bytes 3145736 | tf_op jit(solution)/shard_map/later/ppermute | solution.py:316
  158.3 30.6 %all-to-all-start.3 = ((f32[32,16,128]{2,1,0:T(8,128)}), f32[32,16,128]{2,1,0:T(8,128)S(1)}, u32[]{:S(2)}, u32[]{:S(2)}) async-start(f32[32,16,128]{2,1,0:T(8,128)} %broadcast_in_dim.8), calls=%async_computation.3 | async-start | bytes 524288 | tf_op jit(solution)/shard_map/sums_all/all_to_all | solution.py:314
  176.7 1.2 copy-start.18
  179.7 0.9 copy-start.25
  (9 other events, 7.1 us)

commit v2 on v1

v2 whole, which is shorter than its diff:
```python
import math

import jax
import jax.numpy as jnp
import numpy as np
from jax import lax
from jax.experimental import pallas as pl
from jax.experimental.pallas import tpu as pltpu
from jax.sharding import PartitionSpec as P

TILE = 1024
LANES = 128
BLOCK_ROWS = 16
MIB = 1024 * 1024


def split(value):
    high = value.astype(jnp.bfloat16)
    low = (value - high.astype(jnp.float32)).astype(jnp.bfloat16)
    return high, low


def wave_table(rows):
    size = 2 * rows
    phase = (np.arange(size)[None, :] * (2 * np.arange(rows)[:, None] + 1)) % (2 * size)
    angle = phase * (math.pi / size)
    return np.concatenate([np.cos(angle), -np.sin(angle)], axis=0)


def halves(table):
    high = table.astype(jnp.bfloat16)
    low = (table - high.astype(np.float64)).astype(jnp.bfloat16)
    return jnp.asarray(np.concatenate([high, low], axis=0))


def mm(left, right):
    return jnp.dot(left, right, preferred_element_type=jnp.float32)


def forward(table, value):
    both = mm(table, value)
    half = both.shape[0] // 2
    return both[:half] + both[half:]


def backward(table, value):
    top, rest = split(value)
    return forward(table, top) + mm(table[: table.shape[0] // 2], rest)


def halved(spec):
    half = spec.shape[0] // 2
    return spec[:half], spec[half:]


def filter_spec(taps, table, per_group):
    tap_count, group_count = taps.shape
    channel = lax.broadcasted_iota(jnp.int32, (group_count, TILE), 1) + pl.program_id(0) * TILE
    group = lax.broadcasted_iota(jnp.int32, (group_count, TILE), 0)
    first = group * per_group
    expand = ((channel >= first) & (channel < first + per_group)).astype(jnp.bfloat16)
    wide = mm(taps, expand).astype(jnp.bfloat16)
    return forward(table[:, :tap_count], wide)


def delayed(query, tail, steps):
    moved = pltpu.roll(query, steps, 0)
    row = lax.broadcasted_iota(jnp.int32, query.shape, 0)
    for index in range(steps):
        source = tail.shape[0] - steps + index
        moved = jnp.where(row == index, tail[source : source + 1], moved)
    return moved


def smoothing(query, tail, short):
    moved = [query] + [delayed(query, tail, offset) for offset in range(1, short.shape[0])]
    return sum(short[offset : offset + 1] * value for offset, value in enumerate(moved)), moved


def pack_kernel(capacity, target_ref, grad_ref, out_ref, block, held, come, leave):
    rows, channels = grad_ref.shape
    slots = out_ref.shape[0]
    parts = channels // TILE
    arriving = []
    for index in range(parts):
        cut = pl.ds(index * TILE, TILE)
        arriving.append(
            pltpu.make_async_copy(grad_ref.at[:, cut], block.at[:, cut], come.at[index])
        )
        arriving[-1].start()

    def leaving(cut, index):
        return pltpu.make_async_copy(held.at[:, cut], out_ref.at[:, cut], leave.at[index])

    wide = jnp.broadcast_to(target_ref[...].astype(jnp.float32), (rows, rows))
    across = wide.astype(jnp.int32)
    down = wide.T.astype(jnp.int32)
    upper = lax.broadcasted_iota(jnp.int32, (rows, rows), 0)
    right = lax.broadcasted_iota(jnp.int32, (rows, rows), 1)
    owner = lax.div(across, rows)
    earlier = (owner == lax.div(down, rows)) & (upper < right)
    rank = jnp.sum(earlier.astype(jnp.float32), axis=0, keepdims=True).astype(jnp.int32)
    slot = owner[:1] * capacity + rank
    placing = (lax.broadcasted_iota(jnp.int32, (slots, rows), 0) == slot).astype(jnp.bfloat16)
    for index, copy in enumerate(arriving):
        cut = pl.ds(index * TILE, TILE)
        copy.wait()
        held[:, cut] = mm(placing, block[:, cut]).astype(jnp.bfloat16)
        leaving(cut, index).start()
    landing = (lax.rem(down, rows) == right).astype(jnp.bfloat16)
    held[:, channels:] = mm(placing, landing).astype(jnp.bfloat16)
    leaving(pl.ds(channels, rows), parts).start()
    for index in range(parts):
        leaving(pl.ds(index * TILE, TILE), index).wait()
    leaving(pl.ds(channels, rows), parts).wait()


def early_kernel(
    per_group,
    own_ref,
    prev_ref,
    taps_ref,
    ft_ref,
    it_ref,
    hidden_ref,
    spec_ref,
):
    spec = forward(ft_ref[...], jnp.concatenate([prev_ref[...], own_ref[...]], axis=0))
    spec_ref[...] = spec
    wave = filter_spec(taps_ref[...], ft_ref, per_group)
    sr, si = halved(spec)
    wr, wi = halved(wave)
    product = jnp.concatenate([sr * wr - si * wi, sr * wi + si * wr], axis=0)
    hidden_ref[...] = backward(it_ref[...], product)


def grad_kernel(
    per_group,
    land_ref,
    recv_ref,
    hidden_ref,
    spec_ref,
    query_ref,
    tail_ref,
    short_ref,
    ft_ref,
    ct_ref,
    hgrad_ref,
    sums_ref,
):
    rows = hgrad_ref.shape[0]
    groups = TILE // per_group
    routed = lax.dot_general(
        land_ref[...],
        recv_ref[...],
        (((0,), (0,)), ((), ())),
        preferred_element_type=jnp.float32,
    )
    query = query_ref[...].astype(jnp.float32)
    tail = tail_ref[...].astype(jnp.float32)
    smoothed, moved = smoothing(query, tail, short_ref[...].astype(jnp.float32))
    hgrad = (routed * smoothed).astype(jnp.bfloat16)
    hgrad_ref[...] = hgrad
    sgrad = routed * hidden_ref[...]
    terms = [jnp.sum(sgrad * value, axis=0, keepdims=True) for value in moved]
    terms.append(jnp.zeros((8 - len(moved), TILE), jnp.float32))
    short_terms = jnp.concatenate(terms, axis=0)
    gr, gi = halved(forward(ft_ref[:, rows:], hgrad))
    pr, pi = halved(spec_ref[...])
    cross = jnp.concatenate([gr * pr + gi * pi, gi * pr - gr * pi], axis=0)
    first = lax.broadcasted_iota(jnp.int32, (TILE, groups), 1) * per_group
    channel = lax.broadcasted_iota(jnp.int32, (TILE, groups), 0)
    member = ((channel >= first) & (channel < first + per_group)).astype(jnp.bfloat16)
    top, rest = split(cross)
    grouped = forward(jnp.concatenate([top, rest], axis=0), member)
    lagged = backward(ct_ref[...], grouped).T
    for part in range(TILE // LANES):
        sums_ref[part, :8] = lagged[8 * part : 8 * part + 8]
        sums_ref[part, 8:] = short_terms[:, part * LANES : (part + 1) * LANES]


def own_kernel(per_group, own_ref, taps_ref, ft_ref, it_ref, part_ref):
    rows = own_ref.shape[0]
    gr, gi = halved(forward(ft_ref[:, :rows], own_ref[...]))
    wr, wi = halved(filter_spec(taps_ref[...], ft_ref, per_group))
    product = jnp.concatenate([gr * wr + gi * wi, gi * wr - gr * wi], axis=0)
    part_ref[...] = backward(it_ref[...], product)


def input_kernel(per_group, part_ref, next_ref, taps_ref, ft_ref, it_ref, out_ref):
    rows = next_ref.shape[0]
    gr, gi = halved(forward(ft_ref[:, rows:], next_ref[...]))
    wr, wi = halved(filter_spec(taps_ref[...], ft_ref, per_group))
    product = jnp.concatenate([gr * wr + gi * wi, gi * wr - gr * wi], axis=0)
    out_ref[...] = (part_ref[...] + backward(it_ref[...], product)).astype(jnp.bfloat16)


def last_kernel(medium_scale, short_scale, sums_ref, medium_ref, short_ref):
    parts = sums_ref.shape[0]
    groups = medium_ref.shape[1]
    medium = sums_ref[:, :8, :].reshape(groups, LANES)
    medium_ref[...] = medium.T * medium_scale
    for part in range(parts):
        short_ref[:, part * LANES : (part + 1) * LANES] = (
            sums_ref[part, 8 : 8 + short_ref.shape[0]] * short_scale
        )


def params(mib):
    return pltpu.CompilerParams(vmem_limit_bytes=mib * MIB)


def cost(flops, moved):
    return pl.CostEstimate(flops=flops, bytes_accessed=moved, transcendentals=0)


def columns(rows):
    return pl.BlockSpec((rows, TILE), lambda step: (0, step))


def whole(array):
    return pl.BlockSpec(array.shape, lambda step: (0,) * array.ndim)


def body(queries, products, packed_grad, packed_target, short_filter, medium_filter):
    query, product = queries[0], products[0]
    rows, channels = product.shape
    group_count = medium_filter.shape[1]
    per_group = channels // group_count
    short_count = short_filter.shape[0]
    shards, copies = lax.axis_size("seq"), lax.axis_size("dp")
    capacity = 2 * rows // shards
    slots = shards * capacity
    width = channels + rows
    steps = channels // TILE
    table = wave_table(rows)
    forth = halves(table)
    first = halves(table.T[:rows] / rows)
    second = halves(table.T[rows:] / rows)
    f32, bf16 = jnp.float32, jnp.bfloat16

    with jax.named_scope("pack"):
        send = pl.pallas_call(
            lambda *refs: pack_kernel(capacity, *refs),
            in_specs=[
                pl.BlockSpec(memory_space=pltpu.VMEM),
                pl.BlockSpec(memory_space=pl.ANY),
            ],
            out_specs=pl.BlockSpec(memory_space=pl.ANY),
            scratch_shapes=[
                pltpu.VMEM((rows, channels), bf16),
                pltpu.VMEM((slots, width), bf16),
                pltpu.SemaphoreType.DMA((steps,)),
                pltpu.SemaphoreType.DMA((steps + 1,)),
            ],
            out_shape=jax.ShapeDtypeStruct((slots, width), bf16),
            compiler_params=params(56),
            cost_estimate=cost(2 * slots * rows * width, 8 * MIB // 2),
        )(packed_target, packed_grad[0])
    with jax.named_scope("route"):
        recv = lax.all_to_all(
            send.reshape(shards, capacity, width), "seq", split_axis=0, concat_axis=0, tiled=True
        ).reshape(slots, width)
    with jax.named_scope("halo"):
        onward = [(index, index + 1) for index in range(shards - 1)]
        prev = lax.ppermute(product, "seq", onward)
    with jax.named_scope("early"):
        hidden, spec = pl.pallas_call(
            lambda *refs: early_kernel(per_group, *refs),
            grid=(steps,),
            in_specs=[
                columns(rows),
                columns(rows),
                whole(medium_filter),
                whole(forth),
                whole(second),
            ],
            out_specs=[columns(rows), columns(2 * rows)],
            out_shape=[
                jax.ShapeDtypeStruct((rows, channels), f32),
                jax.ShapeDtypeStruct((2 * rows, channels), f32),
            ],
            compiler_params=params(56),
            cost_estimate=cost(10**14, 12 * MIB),
        )(product, prev, medium_filter, forth, second)
    with jax.named_scope("tail"):
        ending, hidden = lax.optimization_barrier((query, hidden))
        tail = lax.ppermute(ending[rows - 16 :], "seq", onward)
    with jax.named_scope("grads"):
        hgrad, sums = pl.pallas_call(
            lambda *refs: grad_kernel(per_group, *refs),
            grid=(steps,),
            in_specs=[
                pl.BlockSpec((slots, rows), lambda step: (0, channels // rows)),
                columns(slots),
                columns(rows),
                columns(2 * rows),
                columns(rows),
                columns(16),
                columns(short_count),
                whole(forth),
                whole(first),
            ],
            out_specs=[
                columns(rows),
                pl.BlockSpec((TILE // LANES, BLOCK_ROWS, LANES), lambda step: (step, 0, 0)),
            ],
            out_shape=[
                jax.ShapeDtypeStruct((rows, channels), bf16),
                jax.ShapeDtypeStruct((channels // LANES, BLOCK_ROWS, LANES), f32),
            ],
            compiler_params=params(56),
            cost_estimate=cost(10 * rows * 2 * rows * channels, 12 * MIB),
        )(recv, recv, hidden, spec, query, tail, short_filter, forth, first)
    with jax.named_scope("sums_seq"):
        mine = jnp.sum(lax.all_to_all(sums, "seq", 0, 0, tiled=True), axis=0)
    with jax.named_scope("own_rows"):
        part = pl.pallas_call(
            lambda *refs: own_kernel(per_group, *refs),
            grid=(steps,),
            in_specs=[columns(rows)] + [whole(medium_filter), whole(forth), whole(first)],
            out_specs=columns(rows),
            out_shape=jax.ShapeDtypeStruct((rows, channels), f32),
            compiler_params=params(56),
            cost_estimate=cost(16 * rows * 2 * rows * channels, 3 * MIB),
        )(hgrad, medium_filter, forth, first)
    with jax.named_scope("later"):
        part, leaving = lax.optimization_barrier((part, hgrad))
        following = lax.ppermute(
            leaving, "seq", [(index + 1, index) for index in range(shards - 1)]
        )
    with jax.named_scope("sums_dp"):
        spread = jnp.broadcast_to(mine[None], (copies, BLOCK_ROWS, LANES))
        mine = jnp.sum(lax.all_to_all(spread, "dp", 0, 0, tiled=True), axis=0)
    with jax.named_scope("input_grad"):
        input_grad = pl.pallas_call(
            lambda *refs: input_kernel(per_group, *refs),
            grid=(steps,),
            in_specs=[columns(rows), columns(rows)]
            + [whole(medium_filter), whole(forth), whole(first)],
            out_specs=columns(rows),
            out_shape=jax.ShapeDtypeStruct((rows, channels), bf16),
            compiler_params=params(56),
            cost_estimate=cost(16 * rows * 2 * rows * channels, 4 * MIB),
        )(part, following, medium_filter, forth, first)
    with jax.named_scope("sums_all"):
        spread = jnp.broadcast_to(mine[None], (shards, BLOCK_ROWS, LANES))
        total = lax.all_to_all(spread, "seq", 0, 0, tiled=True)
    with jax.named_scope("finish"):
        positions = copies * shards * rows
        medium_scale = 1.0 / math.sqrt(positions * per_group)
        short_scale = 1.0 / math.sqrt(positions)
        medium_grad, short_grad = pl.pallas_call(
            lambda *refs: last_kernel(medium_scale, short_scale, *refs),
            out_shape=[
                jax.ShapeDtypeStruct((rows, group_count), f32),
                jax.ShapeDtypeStruct((short_count, channels), f32),
            ],
            compiler_params=params(56),
        )(total)
    return input_grad[None], medium_grad, short_grad


def solution(mesh):
    in_specs = (
        P("dp", "seq", None),
        P("dp", "seq", None),
        P("dp", "seq", None),
        P("dp", "seq"),
        P(),
        P(),
    )
    out_specs = (P("dp", "seq", None), P(), P())
    return jax.shard_map(body, mesh=mesh, in_specs=in_specs, out_specs=out_specs, check_vma=False)
```

time: 192 us -> 149 us (0.78)
  the two profiles are of different devices: /device:TPU:11 before, /device:TPU:1 now
where the time goes in v2:
time: 149 us; the launch traced here: 148 us
  waiting for transfers between devices  49 us (33%)
  starting transfers between devices  42.4 us (28%)
  Pallas kernels  35.4 us (24%)
  blocking collectives  15.8 us (11%)
  local copies, waits for them, and re-layouts  4.98 us (3%)
    ppermute x1, waiting for transfers between devices, body(): tail = lax.ppermute(ending[rows - 16:], 'seq', onward)  22.7 us
    all_to_all x1, starting transfers between devices, body(): mine = jnp.sum(lax.all_to_all(spread, 'dp', 0, 0, tiled=True), axis=0)  16.8 us
    all_to_all x1, waiting for transfers between devices, body(): lax.all_to_all(send.reshape(shards, capacity, width), 'seq', split_axis=0...  15.8 us
    all_to_all x1, blocking collectives, body(): mine = jnp.sum(lax.all_to_all(sums, 'seq', 0, 0, tiled=True), axis=0)  15.8 us
    pallas_call x1, Pallas kernels, body(): pl.pallas_call(lambda *refs: grad_kernel(per_group, *refs), grid=(steps,)...  8.79 us
    all_to_all x1, starting transfers between devices, body(): lax.all_to_all(send.reshape(shards, capacity, width), 'seq', split_axis=0...  7.69 us
    pallas_call x1, Pallas kernels, body(): pl.pallas_call(lambda *refs: early_kernel(per_group, *refs), grid=(steps,...  7.33 us
    pallas_call x1, Pallas kernels, body(): pl.pallas_call(lambda *refs: own_kernel(per_group, *refs), grid=(steps,),...  6.94 us
  transfers between devices with their start and end apart: 6, of which 6 were waited for; matrix products, arithmetic and copies ran while one was open for 1% of the time, Pallas kernels for 17%

profile of v2, /device:TPU:1, one launch (start us, length us, event | category | flops | bytes accessed | tf_op | source)
XLA Modules:
  0.0 148.3 jit_solution(7491383964588756337)
XLA Ops:
  0.6 4.9 %collective-permute-start = (bf16[128,4096]{1,0:T(8,128)(2,1)}, bf16[128,4096]{1,0:T(8,128)(2,1)S(1)}, u32[]{:S(2)}, u32[]{:S(2)}) collective-permute-start(bf16[128,4096]{1,0:T(8,128)(2,1)} %bitcast.10), channel_id=1, source_target_pairs={{0,1},{1,2},{2,3},{3,4},{4,5},{5,6},{6,7},{7,8},{8,9},{9,10},{10,1... | collective-permute-start | bytes 3145736 | tf_op jit(solution)/shard_map/halo/ppermute | solution.py:266
  5.6 3.7 %pack.1 = bf16[256,4224]{1,0:T(8,128)(2,1)} custom-call(s32[1,128]{1,0:T(1,128)} %refs_0_.1, bf16[128,4096]{1,0:T(8,128)(2,1)} %bitcast.9), custom_call_target="tpu_custom_call" | custom-call | flops 276824064 | bytes 4194304 | tf_op jit(solution)/shard_map/pack/pallas_call | solution.py:243
  9.3 7.7 %all-to-all-start = ((bf16[32,8,4224]{2,1,0:T(8,128)(2,1)}), bf16[32,8,4224]{2,1,0:T(8,128)(2,1)}, u32[]{:S(2)}, u32[]{:S(2)}) async-start(bf16[32,8,4224]{2,1,0:T(8,128)(2,1)} %bitcast.6), calls=%async_computation | async-start | bytes 4325376 | tf_op jit(solution)/shard_map/route/all_to_all | solution.py:261
  17.0 0.6 collective-permute-done.refs_1_
  17.6 1.0 copy-done.4
  18.6 7.3 %early.1 = (f32[128,4096]{1,0:T(8,128)}, f32[256,4096]{1,0:T(8,128)}) custom-call(bf16[128,4096]{1,0:T(8,128)(2,1)} %bitcast.11, bf16[128,4096]{1,0:T(8,128)(2,1)} %copy-done.4, bf16[128,256]{1,0:T(8,128)(2,1)} %refs_2_.4, bf16[512,256]{1,0:T(8,128)(2,1)} %constant.8.clone.refs_3_.refs_7_.refs_2_, bf16[256,256]{1,0:T(8,128)(2,1)} %constant.10.clone.refs_4_), custom_call_target="tpu_custom_call" | custom-call | flops 100000000376832 | bytes 12582912 | tf_op jit(solution)/shard_map/early/pallas_call | solution.py:268
  25.9 0.9 slice.3
  26.8 4.3 %collective-permute-start.1 = (bf16[16,4096]{1,0:T(8,128)(2,1)S(1)}, bf16[16,4096]{1,0:T(8,128)(2,1)S(1)}, u32[]{:S(2)}, u32[]{:S(2)}) collective-permute-start(bf16[16,4096]{1,0:T(8,128)(2,1)S(1)} %slice.3), channel_id=1, source_target_pairs={{0,1},{1,2},{2,3},{3,4},{4,5},{5,6},{6,7},{7,8},{8,9},{9,10},{10,1... | collective-permute-start | bytes 393224 | tf_op jit(solution)/shard_map/tail/ppermute | solution.py:288
  31.1 22.7 %collective-permute-done.1.refs_5_ = bf16[16,4096]{1,0:T(8,128)(2,1)S(1)} collective-permute-done((bf16[16,4096]{1,0:T(8,128)(2,1)S(1)}, bf16[16,4096]{1,0:T(8,128)(2,1)S(1)}, u32[]{:S(2)}, u32[]{:S(2)}) %collective-permute-start.1) | collective-permute-done | bytes 131104 | tf_op jit(solution)/shard_map/tail/ppermute | solution.py:288
  53.9 15.8 %all-to-all-done = bf16[32,8,4224]{2,1,0:T(8,128)(2,1)} async-done(((bf16[32,8,4224]{2,1,0:T(8,128)(2,1)}), bf16[32,8,4224]{2,1,0:T(8,128)(2,1)}, u32[]{:S(2)}, u32[]{:S(2)}) %all-to-all-start) | async-done | bytes 2162720 | tf_op jit(solution)/shard_map/route/all_to_all | solution.py:261
  69.7 8.8 %grads.1 = (bf16[128,4096]{1,0:T(8,128)(2,1)}, f32[32,16,128]{2,1,0:T(8,128)}) custom-call(bf16[256,4224]{1,0:T(8,128)(2,1)} %bitcast.2.refs_0_.refs_1_, bf16[256,4224]{1,0:T(8,128)(2,1)} %bitcast.2.refs_0_.refs_1_, f32[128,4096]{1,0:T(8,128)} %get-tuple-element.14.refs_2_, f32[256,4096]{1,0:T(8,128)} %get-tuple-element.15.refs_3_, ...), custom_call_target="tpu_custom_call" | custom-call | flops 1342177280 | bytes 12582912 | tf_op jit(solution)/shard_map/grads/pallas_call | solution.py:290
  78.5 15.8 %all_to_all.20 = f32[32,16,128]{2,1,0:T(8,128)S(1)} all-to-all(f32[32,16,128]{2,1,0:T(8,128)} %get-tuple-element.20), channel_id=1, replica_groups=mesh['dp'=16,'seq'=32] {'seq'}, dimensions={0} | all-to-all | bytes 524288 | tf_op jit(solution)/shard_map/sums_seq/all_to_all | solution.py:316
  94.3 0.7 broadcast_in_dim.7
  95.0 16.8 %all-to-all-start.2 = ((f32[16,16,128]{2,1,0:T(8,128)}), f32[16,16,128]{2,1,0:T(8,128)S(1)}, u32[]{:S(2)}, u32[]{:S(2)}) async-start(f32[16,16,128]{2,1,0:T(8,128)} %broadcast_in_dim.7), calls=%async_computation.2 | async-start | bytes 262144 | tf_op jit(solution)/shard_map/sums_dp/all_to_all | solution.py:334
  111.8 6.9 %own_rows.1.refs_0_ = f32[128,4096]{1,0:T(8,128)} custom-call(bf16[128,4096]{1,0:T(8,128)(2,1)} %get-tuple-element.19.refs_0_, bf16[128,256]{1,0:T(8,128)(2,1)} %refs_2_.4, bf16[512,256]{1,0:T(8,128)(2,1)} %constant.8.clone.refs_3_.refs_7_.refs_2_, bf16[256,256]{1,0:T(8,128)(2,1)} %constant.9.clone.refs_8_.refs_3_.refs_4_), custom_call_target="tpu_custom_call" | custom-call | flops 2147483648 | bytes 3145728 | tf_op jit(solution)/shard_map/own_rows/pallas_call | solution.py:318
  118.7 2.2 %collective-permute-start.2 = (bf16[128,4096]{1,0:T(8,128)(2,1)S(1)}, bf16[128,4096]{1,0:T(8,128)(2,1)S(1)}, u32[]{:S(2)}, u32[]{:S(2)}) collective-permute-start(bf16[128,4096]{1,0:T(8,128)(2,1)S(1)} %copy-done.2), channel_id=1, source_target_pairs={{1,0},{2,1},{3,2},{4,3},{5,4},{6,5},{7,6},{8,7},{9,8},{10,9},{11,1... | collective-permute-start | bytes 3145736 | tf_op jit(solution)/shard_map/later/ppermute | solution.py:329
  121.0 6.4 %all-to-all-done.2 = f32[16,16,128]{2,1,0:T(8,128)S(1)} async-done(((f32[16,16,128]{2,1,0:T(8,128)}), f32[16,16,128]{2,1,0:T(8,128)S(1)}, u32[]{:S(2)}, u32[]{:S(2)}) %all-to-all-start.2) | async-done | bytes 131104 | tf_op jit(solution)/shard_map/sums_dp/all_to_all | solution.py:334
  127.4 0.7 broadcast_in_dim.8
  128.1 6.5 %all-to-all-start.3 = ((f32[32,16,128]{2,1,0:T(8,128)}), f32[32,16,128]{2,1,0:T(8,128)S(1)}, u32[]{:S(2)}, u32[]{:S(2)}) async-start(f32[32,16,128]{2,1,0:T(8,128)} %broadcast_in_dim.8), calls=%async_computation.3 | async-start | bytes 524288 | tf_op jit(solution)/shard_map/sums_all/all_to_all | solution.py:348
  134.8 1.0 copy-done.3
  135.8 6.9 %input_grad.1 = bf16[128,4096]{1,0:T(8,128)(2,1)} custom-call(f32[128,4096]{1,0:T(8,128)} %own_rows.1.refs_0_, bf16[128,4096]{1,0:T(8,128)(2,1)} %copy-done.3, bf16[128,256]{1,0:T(8,128)(2,1)} %refs_2_.4, bf16[512,256]{1,0:T(8,128)(2,1)} %constant.8.clone.refs_3_.refs_7_.refs_2_, bf16[256,256]{1,0:T(8,128)(2,1)} %constant.9.clone.refs_8_.refs_3_.refs_4_), custom_call_target="tpu_custom_call" | custom-call | flops 2147483648 | bytes 4194304 | tf_op jit(solution)/shard_map/input_grad/pallas_call | solution.py:336
  142.8 3.1 %all-to-all-done.3.refs_0_ = f32[32,16,128]{2,1,0:T(8,128)S(1)} async-done(((f32[32,16,128]{2,1,0:T(8,128)}), f32[32,16,128]{2,1,0:T(8,128)S(1)}, u32[]{:S(2)}, u32[]{:S(2)}) %all-to-all-start.3) | async-done | bytes 262176 | tf_op jit(solution)/shard_map/sums_all/all_to_all | solution.py:348
  145.9 0.7 copy-done
  146.6 1.7 %finish.1 = (f32[128,256]{1,0:T(8,128)}, f32[3,4096]{1,0:T(4,128)}) custom-call(f32[32,16,128]{2,1,0:T(8,128)} %copy-done), custom_call_target="tpu_custom_call" | custom-call | tf_op jit(solution)/shard_map/finish/pallas_call | solution.py:353
  (10 shorter events, 0.3 us)
Async XLA Ops:
  0.6 17.0 %collective-permute-start = (bf16[128,4096]{1,0:T(8,128)(2,1)}, bf16[128,4096]{1,0:T(8,128)(2,1)S(1)}, u32[]{:S(2)}, u32[]{:S(2)}) collective-permute-start(bf16[128,4096]{1,0:T(8,128)(2,1)} %bitcast.10), channel_id=1, source_target_pairs={{0,1},{1,2},{2,3},{3,4},{4,5},{5,6},{6,7},{7,8},{8,9},{9,10},{10,1... | collective-permute-start | bytes 3145736 | tf_op jit(solution)/shard_map/halo/ppermute | solution.py:266
  9.3 60.4 %all-to-all-start = ((bf16[32,8,4224]{2,1,0:T(8,128)(2,1)}), bf16[32,8,4224]{2,1,0:T(8,128)(2,1)}, u32[]{:S(2)}, u32[]{:S(2)}) async-start(bf16[32,8,4224]{2,1,0:T(8,128)(2,1)} %bitcast.6), calls=%async_computation | async-start | bytes 4325376 | tf_op jit(solution)/shard_map/route/all_to_all | solution.py:261
  17.6 1.0 copy-start.4
  26.8 27.0 %collective-permute-start.1 = (bf16[16,4096]{1,0:T(8,128)(2,1)S(1)}, bf16[16,4096]{1,0:T(8,128)(2,1)S(1)}, u32[]{:S(2)}, u32[]{:S(2)}) collective-permute-start(bf16[16,4096]{1,0:T(8,128)(2,1)S(1)} %slice.3), channel_id=1, source_target_pairs={{0,1},{1,2},{2,3},{3,4},{4,5},{5,6},{6,7},{7,8},{8,9},{9,10},{10,1... | collective-permute-start | bytes 393224 | tf_op jit(solution)/shard_map/tail/ppermute | solution.py:288
  53.9 15.8 %copy-start.1 = (bf16[16,4096]{1,0:T(8,128)(2,1)}, bf16[16,4096]{1,0:T(8,128)(2,1)S(1)}, u32[]{:S(2)}) copy-start(bf16[16,4096]{1,0:T(8,128)(2,1)S(1)} %collective-permute-done.1.refs_5_) | copy-start | bytes 393220
  95.0 32.4 %all-to-all-start.2 = ((f32[16,16,128]{2,1,0:T(8,128)}), f32[16,16,128]{2,1,0:T(8,128)S(1)}, u32[]{:S(2)}, u32[]{:S(2)}) async-start(f32[16,16,128]{2,1,0:T(8,128)} %broadcast_in_dim.7), calls=%async_computation.2 | async-start | bytes 262144 | tf_op jit(solution)/shard_map/sums_dp/all_to_all | solution.py:334
  111.8 7.0 %copy-start.2 = (bf16[128,4096]{1,0:T(8,128)(2,1)S(1)}, bf16[128,4096]{1,0:T(8,128)(2,1)}, u32[]{:S(2)}) copy-start(bf16[128,4096]{1,0:T(8,128)(2,1)} %get-tuple-element.19.refs_0_) | copy-start | bytes 3145732
  118.7 16.1 %collective-permute-start.2 = (bf16[128,4096]{1,0:T(8,128)(2,1)S(1)}, bf16[128,4096]{1,0:T(8,128)(2,1)S(1)}, u32[]{:S(2)}, u32[]{:S(2)}) collective-permute-start(bf16[128,4096]{1,0:T(8,128)(2,1)S(1)} %copy-done.2), channel_id=1, source_target_pairs={{1,0},{2,1},{3,2},{4,3},{5,4},{6,5},{7,6},{8,7},{9,8},{10,9},{11,1... | collective-permute-start | bytes 3145736 | tf_op jit(solution)/shard_map/later/ppermute | solution.py:329
  128.1 17.7 %all-to-all-start.3 = ((f32[32,16,128]{2,1,0:T(8,128)}), f32[32,16,128]{2,1,0:T(8,128)S(1)}, u32[]{:S(2)}, u32[]{:S(2)}) async-start(f32[32,16,128]{2,1,0:T(8,128)} %broadcast_in_dim.8), calls=%async_computation.3 | async-start | bytes 524288 | tf_op jit(solution)/shard_map/sums_all/all_to_all | solution.py:348
  134.8 1.0 copy-start.3
  145.8 0.7 copy-start

commit v3 on v2

--- a/solution.py
+++ b/solution.py
@@ -9,6 +9,7 @@
 from jax.sharding import PartitionSpec as P
 
 TILE = 1024
+WIDE = 2048
 LANES = 128
 BLOCK_ROWS = 16
 MIB = 1024 * 1024
@@ -33,6 +34,11 @@
     return jnp.asarray(np.concatenate([high, low], axis=0))
 
 
+def beside(table, start, stop):
+    half = table.shape[0] // 2
+    return jnp.concatenate([table[:half, start:stop], table[half:, start:stop]], axis=1)
+
+
 def mm(left, right):
     return jnp.dot(left, right, preferred_element_type=jnp.float32)
 
@@ -43,6 +49,10 @@
     return both[:half] + both[half:]
 
 
+def narrow(table, value):
+    return mm(table, jnp.concatenate([value, value], axis=0))
+
+
 def backward(table, value):
     top, rest = split(value)
     return forward(table, top) + mm(table[: table.shape[0] // 2], rest)
@@ -53,14 +63,14 @@
     return spec[:half], spec[half:]
 
 
-def filter_spec(taps, table, per_group):
-    tap_count, group_count = taps.shape
-    channel = lax.broadcasted_iota(jnp.int32, (group_count, TILE), 1) + pl.program_id(0) * TILE
-    group = lax.broadcasted_iota(jnp.int32, (group_count, TILE), 0)
+def filter_spec(taps, table, per_group, tile):
+    group_count = taps.shape[1]
+    channel = lax.broadcasted_iota(jnp.int32, (group_count, tile), 1) + pl.program_id(0) * tile
+    group = lax.broadcasted_iota(jnp.int32, (group_count, tile), 0)
     first = group * per_group
     expand = ((channel >= first) & (channel < first + per_group)).astype(jnp.bfloat16)
     wide = mm(taps, expand).astype(jnp.bfloat16)
-    return forward(table[:, :tap_count], wide)
+    return narrow(table, wide)
 
 
 def delayed(query, tail, steps):
@@ -121,13 +131,14 @@
     prev_ref,
     taps_ref,
     ft_ref,
+    fn_ref,
     it_ref,
     hidden_ref,
     spec_ref,
 ):
     spec = forward(ft_ref[...], jnp.concatenate([prev_ref[...], own_ref[...]], axis=0))
     spec_ref[...] = spec
-    wave = filter_spec(taps_ref[...], ft_ref, per_group)
+    wave = filter_spec(taps_ref[...], fn_ref[...], per_group, own_ref.shape[1])
     sr, si = halved(spec)
     wr, wi = halved(wave)
     product = jnp.concatenate([sr * wr - si * wi, sr * wi + si * wr], axis=0)
@@ -143,13 +154,13 @@
     query_ref,
     tail_ref,
     short_ref,
-    ft_ref,
+    fn_ref,
     ct_ref,
     hgrad_ref,
     sums_ref,
 ):
-    rows = hgrad_ref.shape[0]
-    groups = TILE // per_group
+    tile = hgrad_ref.shape[1]
+    groups = tile // per_group
     routed = lax.dot_general(
         land_ref[...],
         recv_ref[...],
@@ -163,34 +174,32 @@
     hgrad_ref[...] = hgrad
     sgrad = routed * hidden_ref[...]
     terms = [jnp.sum(sgrad * value, axis=0, keepdims=True) for value in moved]
-    terms.append(jnp.zeros((8 - len(moved), TILE), jnp.float32))
+    terms.append(jnp.zeros((8 - len(moved), tile), jnp.float32))
     short_terms = jnp.concatenate(terms, axis=0)
-    gr, gi = halved(forward(ft_ref[:, rows:], hgrad))
+    gr, gi = halved(narrow(fn_ref[...], hgrad))
     pr, pi = halved(spec_ref[...])
     cross = jnp.concatenate([gr * pr + gi * pi, gi * pr - gr * pi], axis=0)
-    first = lax.broadcasted_iota(jnp.int32, (TILE, groups), 1) * per_group
-    channel = lax.broadcasted_iota(jnp.int32, (TILE, groups), 0)
+    first = lax.broadcasted_iota(jnp.int32, (tile, groups), 1) * per_group
+    channel = lax.broadcasted_iota(jnp.int32, (tile, groups), 0)
     member = ((channel >= first) & (channel < first + per_group)).astype(jnp.bfloat16)
     top, rest = split(cross)
     grouped = forward(jnp.concatenate([top, rest], axis=0), member)
     lagged = backward(ct_ref[...], grouped).T
-    for part in range(TILE // LANES):
+    for part in range(tile // LANES):
         sums_ref[part, :8] = lagged[8 * part : 8 * part + 8]
         sums_ref[part, 8:] = short_terms[:, part * LANES : (part + 1) * LANES]
 
 
-def own_kernel(per_group, own_ref, taps_ref, ft_ref, it_ref, part_ref):
-    rows = own_ref.shape[0]
-    gr, gi = halved(forward(ft_ref[:, :rows], own_ref[...]))
-    wr, wi = halved(filter_spec(taps_ref[...], ft_ref, per_group))
+def own_kernel(per_group, own_ref, taps_ref, fn_ref, it_ref, part_ref):
+    gr, gi = halved(narrow(fn_ref[...], own_ref[...]))
+    wr, wi = halved(filter_spec(taps_ref[...], fn_ref[...], per_group, own_ref.shape[1]))
     product = jnp.concatenate([gr * wr + gi * wi, gi * wr - gr * wi], axis=0)
     part_ref[...] = backward(it_ref[...], product)
 
 
-def input_kernel(per_group, part_ref, next_ref, taps_ref, ft_ref, it_ref, out_ref):
-    rows = next_ref.shape[0]
-    gr, gi = halved(forward(ft_ref[:, rows:], next_ref[...]))
-    wr, wi = halved(filter_spec(taps_ref[...], ft_ref, per_group))
+def input_kernel(per_group, part_ref, next_ref, taps_ref, fn_ref, gn_ref, it_ref, out_ref):
+    gr, gi = halved(narrow(gn_ref[...], next_ref[...]))
+    wr, wi = halved(filter_spec(taps_ref[...], fn_ref[...], per_group, next_ref.shape[1]))
     product = jnp.concatenate([gr * wr + gi * wi, gi * wr - gr * wi], axis=0)
     out_ref[...] = (part_ref[...] + backward(it_ref[...], product)).astype(jnp.bfloat16)
 
@@ -214,8 +223,8 @@
     return pl.CostEstimate(flops=flops, bytes_accessed=moved, transcendentals=0)
 
 
-def columns(rows):
-    return pl.BlockSpec((rows, TILE), lambda step: (0, step))
+def columns(rows, tile=WIDE):
+    return pl.BlockSpec((rows, tile), lambda step: (0, step))
 
 
 def whole(array):
@@ -232,9 +241,12 @@
     capacity = 2 * rows // shards
     slots = shards * capacity
     width = channels + rows
-    steps = channels // TILE
+    chunks = channels // TILE
+    steps = channels // WIDE
     table = wave_table(rows)
     forth = halves(table)
+    lower = beside(forth, 0, rows)
+    upper = beside(forth, rows, 2 * rows)
     first = halves(table.T[:rows] / rows)
     second = halves(table.T[rows:] / rows)
     f32, bf16 = jnp.float32, jnp.bfloat16
@@ -250,11 +262,11 @@
             scratch_shapes=[
                 pltpu.VMEM((rows, channels), bf16),
                 pltpu.VMEM((slots, width), bf16),
-                pltpu.SemaphoreType.DMA((steps,)),
-                pltpu.SemaphoreType.DMA((steps + 1,)),
+                pltpu.SemaphoreType.DMA((chunks,)),
+                pltpu.SemaphoreType.DMA((chunks + 1,)),
             ],
             out_shape=jax.ShapeDtypeStruct((slots, width), bf16),
-            compiler_params=params(56),
+            compiler_params=params(60),
             cost_estimate=cost(2 * slots * rows * width, 8 * MIB // 2),
         )(packed_target, packed_grad[0])
     with jax.named_scope("route"):
@@ -273,6 +285,7 @@
                 columns(rows),
                 whole(medium_filter),
                 whole(forth),
+                whole(lower),
                 whole(second),
             ],
             out_specs=[columns(rows), columns(2 * rows)],
@@ -280,9 +293,9 @@
                 jax.ShapeDtypeStruct((rows, channels), f32),
                 jax.ShapeDtypeStruct((2 * rows, channels), f32),
             ],
-            compiler_params=params(56),
+            compiler_params=params(60),
             cost_estimate=cost(10**14, 12 * MIB),
-        )(product, prev, medium_filter, forth, second)
+        )(product, prev, medium_filter, forth, lower, second)
     with jax.named_scope("tail"):
         ending, hidden = lax.optimization_barrier((query, hidden))
         tail = lax.ppermute(ending[rows - 16 :], "seq", onward)
@@ -298,32 +311,32 @@
                 columns(rows),
                 columns(16),
                 columns(short_count),
-                whole(forth),
+                whole(upper),
                 whole(first),
             ],
             out_specs=[
                 columns(rows),
-                pl.BlockSpec((TILE // LANES, BLOCK_ROWS, LANES), lambda step: (step, 0, 0)),
+                pl.BlockSpec((WIDE // LANES, BLOCK_ROWS, LANES), lambda step: (step, 0, 0)),
             ],
             out_shape=[
                 jax.ShapeDtypeStruct((rows, channels), bf16),
                 jax.ShapeDtypeStruct((channels // LANES, BLOCK_ROWS, LANES), f32),
             ],
-            compiler_params=params(56),
+            compiler_params=params(60),
             cost_estimate=cost(10 * rows * 2 * rows * channels, 12 * MIB),
-        )(recv, recv, hidden, spec, query, tail, short_filter, forth, first)
+        )(recv, recv, hidden, spec, query, tail, short_filter, upper, first)
     with jax.named_scope("sums_seq"):
         mine = jnp.sum(lax.all_to_all(sums, "seq", 0, 0, tiled=True), axis=0)
     with jax.named_scope("own_rows"):
         part = pl.pallas_call(
             lambda *refs: own_kernel(per_group, *refs),
             grid=(steps,),
-            in_specs=[columns(rows)] + [whole(medium_filter), whole(forth), whole(first)],
+            in_specs=[columns(rows)] + [whole(medium_filter), whole(lower), whole(first)],
             out_specs=columns(rows),
             out_shape=jax.ShapeDtypeStruct((rows, channels), f32),
-            compiler_params=params(56),
+            compiler_params=params(60),
             cost_estimate=cost(16 * rows * 2 * rows * channels, 3 * MIB),
-        )(hgrad, medium_filter, forth, first)
+        )(hgrad, medium_filter, lower, first)
     with jax.named_scope("later"):
         part, leaving = lax.optimization_barrier((part, hgrad))
         following = lax.ppermute(
@@ -337,12 +350,12 @@
             lambda *refs: input_kernel(per_group, *refs),
             grid=(steps,),
             in_specs=[columns(rows), columns(rows)]
-            + [whole(medium_filter), whole(forth), whole(first)],
+            + [whole(medium_filter), whole(lower), whole(upper), whole(first)],
             out_specs=columns(rows),
             out_shape=jax.ShapeDtypeStruct((rows, channels), bf16),
-            compiler_params=params(56),
+            compiler_params=params(60),
             cost_estimate=cost(16 * rows * 2 * rows * channels, 4 * MIB),
-        )(part, following, medium_filter, forth, first)
+        )(part, following, medium_filter, lower, upper, first)
     with jax.named_scope("sums_all"):
         spread = jnp.broadcast_to(mine[None], (shards, BLOCK_ROWS, LANES))
         total = lax.all_to_all(spread, "seq", 0, 0, tiled=True)
@@ -356,7 +369,7 @@
                 jax.ShapeDtypeStruct((rows, group_count), f32),
                 jax.ShapeDtypeStruct((short_count, channels), f32),
             ],
-            compiler_params=params(56),
+            compiler_params=params(8),
         )(total)
     return input_grad[None], medium_grad, short_grad
 

time: 149 us -> 146 us (0.980)
  Pallas kernels: 35.4 us -> 29.6 us
  waiting for transfers between devices: 49 us -> 52.8 us
    all_to_all x1, waiting for transfers between devices: 3.09 us -> 4.76 us  [body(): total = lax.all_to_all(spread, 'seq', 0, 0, tiled=True)]
    pallas_call x1, Pallas kernels: 6.94 us -> 5.43 us  [body(): pl.pallas_call(lambda *refs: own_kernel(per_group, *refs), grid=(steps,),...]
    all_to_all x1, waiting for transfers between devices: 6.39 us -> 7.9 us  [body(): mine = jnp.sum(lax.all_to_all(spread, 'dp', 0, 0, tiled=True), axis=0)]
  transfers between devices with their start and end apart: 6 -> 6, of which waited for: 6 -> 5; matrix products, arithmetic and copies ran while one was open for 1% -> 1% of each run, Pallas kernels for 17% -> 14%
where the time goes in v3:
time: 146 us
  waiting for transfers between devices  52.8 us (36%)
  starting transfers between devices  42.4 us (29%)
  Pallas kernels  29.6 us (20%)
  blocking collectives  15.7 us (11%)
  local copies, waits for them, and re-layouts  4.26 us (3%)
    ppermute x1, waiting for transfers between devices, body(): tail = lax.ppermute(ending[rows - 16:], 'seq', onward)  23.7 us
    all_to_all x1, starting transfers between devices, body(): mine = jnp.sum(lax.all_to_all(spread, 'dp', 0, 0, tiled=True), axis=0)  16.8 us
    all_to_all x1, waiting for transfers between devices, body(): lax.all_to_all(send.reshape(shards, capacity, width), 'seq', split_axis=0...  15.8 us
    all_to_all x1, blocking collectives, body(): mine = jnp.sum(lax.all_to_all(sums, 'seq', 0, 0, tiled=True), axis=0)  15.7 us
    all_to_all x1, waiting for transfers between devices, body(): mine = jnp.sum(lax.all_to_all(spread, 'dp', 0, 0, tiled=True), axis=0)  7.9 us
    pallas_call x1, Pallas kernels, body(): pl.pallas_call(lambda *refs: grad_kernel(per_group, *refs), grid=(steps,)...  7.85 us
    all_to_all x1, starting transfers between devices, body(): lax.all_to_all(send.reshape(shards, capacity, width), 'seq', split_axis=0...  7.7 us
    all_to_all x1, starting transfers between devices, body(): total = lax.all_to_all(spread, 'seq', 0, 0, tiled=True)  6.45 us
  transfers between devices with their start and end apart: 6, of which 5 were waited for; matrix products, arithmetic and copies ran while one was open for 1% of the time, Pallas kernels for 14%

profile of v3, /device:TPU:1, one launch (start us, length us, event | category | flops | bytes accessed | tf_op | source)
XLA Modules:
  0.0 145.7 jit_solution(221377977980285816)
XLA Ops:
  0.6 4.9 %collective-permute-start = (bf16[128,4096]{1,0:T(8,128)(2,1)}, bf16[128,4096]{1,0:T(8,128)(2,1)S(1)}, u32[]{:S(2)}, u32[]{:S(2)}) collective-permute-start(bf16[128,4096]{1,0:T(8,128)(2,1)} %bitcast.10), channel_id=1, source_target_pairs={{0,1},{1,2},{2,3},{3,4},{4,5},{5,6},{6,7},{7,8},{8,9},{9,10},{10,1... | collective-permute-start | bytes 3145736 | tf_op jit(solution)/shard_map/halo/ppermute | solution.py:278
  5.6 3.7 %pack.1 = bf16[256,4224]{1,0:T(8,128)(2,1)} custom-call(s32[1,128]{1,0:T(1,128)} %refs_0_.1, bf16[128,4096]{1,0:T(8,128)(2,1)} %bitcast.9), custom_call_target="tpu_custom_call" | custom-call | flops 276824064 | bytes 4194304 | tf_op jit(solution)/shard_map/pack/pallas_call | solution.py:255
  9.3 7.7 %all-to-all-start = ((bf16[32,8,4224]{2,1,0:T(8,128)(2,1)}), bf16[32,8,4224]{2,1,0:T(8,128)(2,1)}, u32[]{:S(2)}, u32[]{:S(2)}) async-start(bf16[32,8,4224]{2,1,0:T(8,128)(2,1)} %bitcast.6), calls=%async_computation | async-start | bytes 4325376 | tf_op jit(solution)/shard_map/route/all_to_all | solution.py:273
  17.0 0.6 collective-permute-done.refs_1_
  17.6 1.0 copy-done.3
  18.6 6.4 %early.1 = (f32[128,4096]{1,0:T(8,128)}, f32[256,4096]{1,0:T(8,128)}) custom-call(bf16[128,4096]{1,0:T(8,128)(2,1)} %bitcast.11, bf16[128,4096]{1,0:T(8,128)(2,1)} %copy-done.3, bf16[128,256]{1,0:T(8,128)(2,1)} %refs_2_.3, bf16[512,256]{1,0:T(8,128)(2,1)} %constant.8.clone.refs_3_, bf16[256,256]{1,0:T(8,128)(2,1)} %constant.17.refs_4_.refs_2_.refs_3_, ...), custom_call_target="tpu_custom_call" | custom-call | flops 100000000376832 | bytes 12582912 | tf_op jit(solution)/shard_map/early/pallas_call | solution.py:280
  24.9 0.9 slice.17
  25.9 4.3 %collective-permute-start.1 = (bf16[16,4096]{1,0:T(8,128)(2,1)S(1)}, bf16[16,4096]{1,0:T(8,128)(2,1)S(1)}, u32[]{:S(2)}, u32[]{:S(2)}) collective-permute-start(bf16[16,4096]{1,0:T(8,128)(2,1)S(1)} %slice.17), channel_id=1, source_target_pairs={{0,1},{1,2},{2,3},{3,4},{4,5},{5,6},{6,7},{7,8},{8,9},{9,10},{10,1... | collective-permute-start | bytes 393224 | tf_op jit(solution)/shard_map/tail/ppermute | solution.py:301
  30.2 23.7 %collective-permute-done.1.refs_5_ = bf16[16,4096]{1,0:T(8,128)(2,1)S(1)} collective-permute-done((bf16[16,4096]{1,0:T(8,128)(2,1)S(1)}, bf16[16,4096]{1,0:T(8,128)(2,1)S(1)}, u32[]{:S(2)}, u32[]{:S(2)}) %collective-permute-start.1) | collective-permute-done | bytes 131104 | tf_op jit(solution)/shard_map/tail/ppermute | solution.py:301
  53.9 15.8 %all-to-all-done = bf16[32,8,4224]{2,1,0:T(8,128)(2,1)} async-done(((bf16[32,8,4224]{2,1,0:T(8,128)(2,1)}), bf16[32,8,4224]{2,1,0:T(8,128)(2,1)}, u32[]{:S(2)}, u32[]{:S(2)}) %all-to-all-start) | async-done | bytes 2162720 | tf_op jit(solution)/shard_map/route/all_to_all | solution.py:273
  69.7 7.9 %grads.1 = (bf16[128,4096]{1,0:T(8,128)(2,1)}, f32[32,16,128]{2,1,0:T(8,128)}) custom-call(bf16[256,4224]{1,0:T(8,128)(2,1)} %bitcast.2.refs_0_.refs_1_, bf16[256,4224]{1,0:T(8,128)(2,1)} %bitcast.2.refs_0_.refs_1_, f32[128,4096]{1,0:T(8,128)} %get-tuple-element.14.refs_2_, f32[256,4096]{1,0:T(8,128)} %get-tuple-element.15.refs_3_, ...), custom_call_target="tpu_custom_call" | custom-call | flops 1342177280 | bytes 12582912 | tf_op jit(solution)/shard_map/grads/pallas_call | solution.py:303
  77.6 15.7 %all_to_all.20 = f32[32,16,128]{2,1,0:T(8,128)S(1)} all-to-all(f32[32,16,128]{2,1,0:T(8,128)} %get-tuple-element.20), channel_id=1, replica_groups=mesh['dp'=16,'seq'=32] {'seq'}, dimensions={0} | all-to-all | bytes 524288 | tf_op jit(solution)/shard_map/sums_seq/all_to_all | solution.py:329
  93.3 0.7 broadcast_in_dim.7
  94.0 16.8 %all-to-all-start.2 = ((f32[16,16,128]{2,1,0:T(8,128)}), f32[16,16,128]{2,1,0:T(8,128)S(1)}, u32[]{:S(2)}, u32[]{:S(2)}) async-start(f32[16,16,128]{2,1,0:T(8,128)} %broadcast_in_dim.7), calls=%async_computation.2 | async-start | bytes 262144 | tf_op jit(solution)/shard_map/sums_dp/all_to_all | solution.py:347
  110.8 0.0 copy-start.1
  110.8 5.4 %own_rows.1.refs_0_ = f32[128,4096]{1,0:T(8,128)} custom-call(bf16[128,4096]{1,0:T(8,128)(2,1)} %get-tuple-element.19.refs_0_, bf16[128,256]{1,0:T(8,128)(2,1)} %refs_2_.3, bf16[256,256]{1,0:T(8,128)(2,1)} %constant.17.refs_4_.refs_2_.refs_3_, bf16[256,256]{1,0:T(8,128)(2,1)} %constant.9.clone.refs_8_.refs_3_.refs_5_), custom_call_target="tpu_custom_call" | custom-call | flops 2147483648 | bytes 3145728 | tf_op jit(solution)/shard_map/own_rows/pallas_call | solution.py:331
  116.3 2.3 %collective-permute-start.2 = (bf16[128,4096]{1,0:T(8,128)(2,1)S(1)}, bf16[128,4096]{1,0:T(8,128)(2,1)S(1)}, u32[]{:S(2)}, u32[]{:S(2)}) collective-permute-start(bf16[128,4096]{1,0:T(8,128)(2,1)S(1)} %copy-done.1), channel_id=1, source_target_pairs={{1,0},{2,1},{3,2},{4,3},{5,4},{6,5},{7,6},{8,7},{9,8},{10,9},{11,1... | collective-permute-start | bytes 3145736 | tf_op jit(solution)/shard_map/later/ppermute | solution.py:342
  118.5 7.9 %all-to-all-done.2 = f32[16,16,128]{2,1,0:T(8,128)S(1)} async-done(((f32[16,16,128]{2,1,0:T(8,128)}), f32[16,16,128]{2,1,0:T(8,128)S(1)}, u32[]{:S(2)}, u32[]{:S(2)}) %all-to-all-start.2) | async-done | bytes 131104 | tf_op jit(solution)/shard_map/sums_dp/all_to_all | solution.py:347
  126.4 0.7 broadcast_in_dim.8
  127.2 6.5 %all-to-all-start.3 = ((f32[32,16,128]{2,1,0:T(8,128)}), f32[32,16,128]{2,1,0:T(8,128)S(1)}, u32[]{:S(2)}, u32[]{:S(2)}) async-start(f32[32,16,128]{2,1,0:T(8,128)} %broadcast_in_dim.8), calls=%async_computation.3 | async-start | bytes 524288 | tf_op jit(solution)/shard_map/sums_all/all_to_all | solution.py:361
  133.6 1.0 copy-done.2
  134.6 5.5 %input_grad.1 = bf16[128,4096]{1,0:T(8,128)(2,1)} custom-call(f32[128,4096]{1,0:T(8,128)} %own_rows.1.refs_0_, bf16[128,4096]{1,0:T(8,128)(2,1)} %copy-done.2, bf16[128,256]{1,0:T(8,128)(2,1)} %refs_2_.3, bf16[256,256]{1,0:T(8,128)(2,1)} %constant.17.refs_4_.refs_2_.refs_3_, bf16[256,256]{1,0:T(8,128)(2,1)} %constant.20.refs_7_.refs_4_, ...), custom_call_target="tpu_custom_call" | custom-call | flops 2147483648 | bytes 4194304 | tf_op jit(solution)/shard_map/input_grad/pallas_call | solution.py:349
  140.1 4.8 %all-to-all-done.3.refs_0_ = f32[32,16,128]{2,1,0:T(8,128)S(1)} async-done(((f32[32,16,128]{2,1,0:T(8,128)}), f32[32,16,128]{2,1,0:T(8,128)S(1)}, u32[]{:S(2)}, u32[]{:S(2)}) %all-to-all-start.3) | async-done | bytes 262176 | tf_op jit(solution)/shard_map/sums_all/all_to_all | solution.py:361
  144.9 0.8 finish.1
  (8 shorter events, 0.1 us)
Async XLA Ops:
  0.6 17.0 %collective-permute-start = (bf16[128,4096]{1,0:T(8,128)(2,1)}, bf16[128,4096]{1,0:T(8,128)(2,1)S(1)}, u32[]{:S(2)}, u32[]{:S(2)}) collective-permute-start(bf16[128,4096]{1,0:T(8,128)(2,1)} %bitcast.10), channel_id=1, source_target_pairs={{0,1},{1,2},{2,3},{3,4},{4,5},{5,6},{6,7},{7,8},{8,9},{9,10},{10,1... | collective-permute-start | bytes 3145736 | tf_op jit(solution)/shard_map/halo/ppermute | solution.py:278
  9.3 60.4 %all-to-all-start = ((bf16[32,8,4224]{2,1,0:T(8,128)(2,1)}), bf16[32,8,4224]{2,1,0:T(8,128)(2,1)}, u32[]{:S(2)}, u32[]{:S(2)}) async-start(bf16[32,8,4224]{2,1,0:T(8,128)(2,1)} %bitcast.6), calls=%async_computation | async-start | bytes 4325376 | tf_op jit(solution)/shard_map/route/all_to_all | solution.py:273
  17.6 1.0 copy-start.3
  25.9 28.0 %collective-permute-start.1 = (bf16[16,4096]{1,0:T(8,128)(2,1)S(1)}, bf16[16,4096]{1,0:T(8,128)(2,1)S(1)}, u32[]{:S(2)}, u32[]{:S(2)}) collective-permute-start(bf16[16,4096]{1,0:T(8,128)(2,1)S(1)} %slice.17), channel_id=1, source_target_pairs={{0,1},{1,2},{2,3},{3,4},{4,5},{5,6},{6,7},{7,8},{8,9},{9,10},{10,1... | collective-permute-start | bytes 393224 | tf_op jit(solution)/shard_map/tail/ppermute | solution.py:301
  53.9 15.8 %copy-start = (bf16[16,4096]{1,0:T(8,128)(2,1)}, bf16[16,4096]{1,0:T(8,128)(2,1)S(1)}, u32[]{:S(2)}) copy-start(bf16[16,4096]{1,0:T(8,128)(2,1)S(1)} %collective-permute-done.1.refs_5_) | copy-start | bytes 393220
  94.0 32.4 %all-to-all-start.2 = ((f32[16,16,128]{2,1,0:T(8,128)}), f32[16,16,128]{2,1,0:T(8,128)S(1)}, u32[]{:S(2)}, u32[]{:S(2)}) async-start(f32[16,16,128]{2,1,0:T(8,128)} %broadcast_in_dim.7), calls=%async_computation.2 | async-start | bytes 262144 | tf_op jit(solution)/shard_map/sums_dp/all_to_all | solution.py:347
  110.8 5.4 %copy-start.1 = (bf16[128,4096]{1,0:T(8,128)(2,1)S(1)}, bf16[128,4096]{1,0:T(8,128)(2,1)}, u32[]{:S(2)}) copy-start(bf16[128,4096]{1,0:T(8,128)(2,1)} %get-tuple-element.19.refs_0_) | copy-start | bytes 3145732
  116.3 17.4 %collective-permute-start.2 = (bf16[128,4096]{1,0:T(8,128)(2,1)S(1)}, bf16[128,4096]{1,0:T(8,128)(2,1)S(1)}, u32[]{:S(2)}, u32[]{:S(2)}) collective-permute-start(bf16[128,4096]{1,0:T(8,128)(2,1)S(1)} %copy-done.1), channel_id=1, source_target_pairs={{1,0},{2,1},{3,2},{4,3},{5,4},{6,5},{7,6},{8,7},{9,8},{10,9},{11,1... | collective-permute-start | bytes 3145736 | tf_op jit(solution)/shard_map/later/ppermute | solution.py:342
  127.2 17.7 %all-to-all-start.3 = ((f32[32,16,128]{2,1,0:T(8,128)}), f32[32,16,128]{2,1,0:T(8,128)S(1)}, u32[]{:S(2)}, u32[]{:S(2)}) async-start(f32[32,16,128]{2,1,0:T(8,128)} %broadcast_in_dim.8), calls=%async_computation.3 | async-start | bytes 524288 | tf_op jit(solution)/shard_map/sums_all/all_to_all | solution.py:361
  133.6 1.0 copy-start.2

commit v4 on v3

--- a/solution.py
+++ b/solution.py
@@ -298,7 +298,7 @@
         )(product, prev, medium_filter, forth, lower, second)
     with jax.named_scope("tail"):
         ending, hidden = lax.optimization_barrier((query, hidden))
-        tail = lax.ppermute(ending[rows - 16 :], "seq", onward)
+        tail = lax.ppermute(ending[rows - short_count + 1 :], "seq", onward)
     with jax.named_scope("grads"):
         hgrad, sums = pl.pallas_call(
             lambda *refs: grad_kernel(per_group, *refs),
@@ -309,7 +309,7 @@
                 columns(rows),
                 columns(2 * rows),
                 columns(rows),
-                columns(16),
+                columns(short_count - 1),
                 columns(short_count),
                 whole(upper),
                 whole(first),

time: 146 us -> 145 us (level)
  transfers between devices with their start and end apart: 6 -> 6, of which waited for: 5 -> 5; matrix products, arithmetic and copies ran while one was open for 1% -> 1% of each run, Pallas kernels for 14% -> 15%
where the time goes in v4:
time: 145 us; the launch traced here: 144 us
  waiting for transfers between devices  51.7 us (36%)
  starting transfers between devices  42.2 us (29%)
  Pallas kernels  29.7 us (20%)
  blocking collectives  15.9 us (11%)
  local copies, waits for them, and re-layouts  4.2 us (3%)
    ppermute x1, waiting for transfers between devices, body(): tail = lax.ppermute(ending[rows - short_count + 1:], 'seq', onward)  22.4 us
    all_to_all x1, starting transfers between devices, body(): mine = jnp.sum(lax.all_to_all(spread, 'dp', 0, 0, tiled=True), axis=0)  16.6 us
    all_to_all x1, waiting for transfers between devices, body(): lax.all_to_all(send.reshape(shards, capacity, width), 'seq', split_axis=0...  16 us
    all_to_all x1, blocking collectives, body(): mine = jnp.sum(lax.all_to_all(sums, 'seq', 0, 0, tiled=True), axis=0)  15.9 us
    all_to_all x1, waiting for transfers between devices, body(): mine = jnp.sum(lax.all_to_all(spread, 'dp', 0, 0, tiled=True), axis=0)  7.9 us
    pallas_call x1, Pallas kernels, body(): pl.pallas_call(lambda *refs: grad_kernel(per_group, *refs), grid=(steps,)...  7.86 us
    all_to_all x1, starting transfers between devices, body(): lax.all_to_all(send.reshape(shards, capacity, width), 'seq', split_axis=0...  7.69 us
    all_to_all x1, starting transfers between devices, body(): total = lax.all_to_all(spread, 'seq', 0, 0, tiled=True)  6.45 us
  transfers between devices with their start and end apart: 6, of which 5 were waited for; matrix products, arithmetic and copies ran while one was open for 1% of the time, Pallas kernels for 15%

profile of v4, /device:TPU:1, one launch (start us, length us, event | category | flops | bytes accessed | tf_op | source)
XLA Modules:
  0.0 144.4 jit_solution(9027502789893051985)
XLA Ops:
  0.6 4.9 %collective-permute-start = (bf16[128,4096]{1,0:T(8,128)(2,1)}, bf16[128,4096]{1,0:T(8,128)(2,1)S(1)}, u32[]{:S(2)}, u32[]{:S(2)}) collective-permute-start(bf16[128,4096]{1,0:T(8,128)(2,1)} %bitcast.10), channel_id=1, source_target_pairs={{0,1},{1,2},{2,3},{3,4},{4,5},{5,6},{6,7},{7,8},{8,9},{9,10},{10,1... | collective-permute-start | bytes 3145736 | tf_op jit(solution)/shard_map/halo/ppermute | solution.py:278
  5.6 3.7 %pack.1 = bf16[256,4224]{1,0:T(8,128)(2,1)} custom-call(s32[1,128]{1,0:T(1,128)} %refs_0_.1, bf16[128,4096]{1,0:T(8,128)(2,1)} %bitcast.9), custom_call_target="tpu_custom_call" | custom-call | flops 276824064 | bytes 4194304 | tf_op jit(solution)/shard_map/pack/pallas_call | solution.py:255
  9.3 7.7 %all-to-all-start = ((bf16[32,8,4224]{2,1,0:T(8,128)(2,1)}), bf16[32,8,4224]{2,1,0:T(8,128)(2,1)}, u32[]{:S(2)}, u32[]{:S(2)}) async-start(bf16[32,8,4224]{2,1,0:T(8,128)(2,1)} %bitcast.6), calls=%async_computation | async-start | bytes 4325376 | tf_op jit(solution)/shard_map/route/all_to_all | solution.py:273
  17.0 0.6 collective-permute-done.refs_1_
  17.6 1.0 copy-done.3
  18.6 6.4 %early.1 = (f32[128,4096]{1,0:T(8,128)}, f32[256,4096]{1,0:T(8,128)}) custom-call(bf16[128,4096]{1,0:T(8,128)(2,1)} %bitcast.11, bf16[128,4096]{1,0:T(8,128)(2,1)} %copy-done.3, bf16[128,256]{1,0:T(8,128)(2,1)} %refs_2_.3, bf16[512,256]{1,0:T(8,128)(2,1)} %constant.8.clone.refs_3_, bf16[256,256]{1,0:T(8,128)(2,1)} %constant.17.refs_4_.refs_2_.refs_3_, ...), custom_call_target="tpu_custom_call" | custom-call | flops 100000000376832 | bytes 12582912 | tf_op jit(solution)/shard_map/early/pallas_call | solution.py:280
  24.9 0.9 slice.17
  25.8 4.3 %collective-permute-start.1 = (bf16[2,4096]{1,0:T(2,128)(2,1)S(1)}, bf16[2,4096]{1,0:T(2,128)(2,1)S(1)}, u32[]{:S(2)}, u32[]{:S(2)}) collective-permute-start(bf16[2,4096]{1,0:T(2,128)(2,1)S(1)} %slice.17), channel_id=1, source_target_pairs={{0,1},{1,2},{2,3},{3,4},{4,5},{5,6},{6,7},{7,8},{8,9},{9,10},{10,1... | collective-permute-start | bytes 49160 | tf_op jit(solution)/shard_map/tail/ppermute | solution.py:301
  30.1 22.4 %collective-permute-done.1.refs_5_ = bf16[2,4096]{1,0:T(2,128)(2,1)S(1)} collective-permute-done((bf16[2,4096]{1,0:T(2,128)(2,1)S(1)}, bf16[2,4096]{1,0:T(2,128)(2,1)S(1)}, u32[]{:S(2)}, u32[]{:S(2)}) %collective-permute-start.1) | collective-permute-done | bytes 16416 | tf_op jit(solution)/shard_map/tail/ppermute | solution.py:301
  52.5 16.0 %all-to-all-done = bf16[32,8,4224]{2,1,0:T(8,128)(2,1)} async-done(((bf16[32,8,4224]{2,1,0:T(8,128)(2,1)}), bf16[32,8,4224]{2,1,0:T(8,128)(2,1)}, u32[]{:S(2)}, u32[]{:S(2)}) %all-to-all-start) | async-done | bytes 2162720 | tf_op jit(solution)/shard_map/route/all_to_all | solution.py:273
  68.6 7.9 %grads.1 = (bf16[128,4096]{1,0:T(8,128)(2,1)}, f32[32,16,128]{2,1,0:T(8,128)}) custom-call(bf16[256,4224]{1,0:T(8,128)(2,1)} %bitcast.2.refs_0_.refs_1_, bf16[256,4224]{1,0:T(8,128)(2,1)} %bitcast.2.refs_0_.refs_1_, f32[128,4096]{1,0:T(8,128)} %get-tuple-element.14.refs_2_, f32[256,4096]{1,0:T(8,128)} %get-tuple-element.15.refs_3_, ...), custom_call_target="tpu_custom_call" | custom-call | flops 1342177280 | bytes 12582912 | tf_op jit(solution)/shard_map/grads/pallas_call | solution.py:303
  76.4 15.9 %all_to_all.20 = f32[32,16,128]{2,1,0:T(8,128)S(1)} all-to-all(f32[32,16,128]{2,1,0:T(8,128)} %get-tuple-element.20), channel_id=1, replica_groups=mesh['dp'=16,'seq'=32] {'seq'}, dimensions={0} | all-to-all | bytes 524288 | tf_op jit(solution)/shard_map/sums_seq/all_to_all | solution.py:329
  92.3 0.7 broadcast_in_dim.7
  93.0 16.6 %all-to-all-start.2 = ((f32[16,16,128]{2,1,0:T(8,128)}), f32[16,16,128]{2,1,0:T(8,128)S(1)}, u32[]{:S(2)}, u32[]{:S(2)}) async-start(f32[16,16,128]{2,1,0:T(8,128)} %broadcast_in_dim.7), calls=%async_computation.2 | async-start | bytes 262144 | tf_op jit(solution)/shard_map/sums_dp/all_to_all | solution.py:347
  109.6 0.0 copy-start.1
  109.6 5.4 %own_rows.1.refs_0_ = f32[128,4096]{1,0:T(8,128)} custom-call(bf16[128,4096]{1,0:T(8,128)(2,1)} %get-tuple-element.19.refs_0_, bf16[128,256]{1,0:T(8,128)(2,1)} %refs_2_.3, bf16[256,256]{1,0:T(8,128)(2,1)} %constant.17.refs_4_.refs_2_.refs_3_, bf16[256,256]{1,0:T(8,128)(2,1)} %constant.9.clone.refs_8_.refs_3_.refs_5_), custom_call_target="tpu_custom_call" | custom-call | flops 2147483648 | bytes 3145728 | tf_op jit(solution)/shard_map/own_rows/pallas_call | solution.py:331
  115.0 2.2 %collective-permute-start.2 = (bf16[128,4096]{1,0:T(8,128)(2,1)S(1)}, bf16[128,4096]{1,0:T(8,128)(2,1)S(1)}, u32[]{:S(2)}, u32[]{:S(2)}) collective-permute-start(bf16[128,4096]{1,0:T(8,128)(2,1)S(1)} %copy-done.1), channel_id=1, source_target_pairs={{1,0},{2,1},{3,2},{4,3},{5,4},{6,5},{7,6},{8,7},{9,8},{10,9},{11,1... | collective-permute-start | bytes 3145736 | tf_op jit(solution)/shard_map/later/ppermute | solution.py:342
  117.3 7.9 %all-to-all-done.2 = f32[16,16,128]{2,1,0:T(8,128)S(1)} async-done(((f32[16,16,128]{2,1,0:T(8,128)}), f32[16,16,128]{2,1,0:T(8,128)S(1)}, u32[]{:S(2)}, u32[]{:S(2)}) %all-to-all-start.2) | async-done | bytes 131104 | tf_op jit(solution)/shard_map/sums_dp/all_to_all | solution.py:347
  125.2 0.7 broadcast_in_dim.8
  125.9 6.4 %all-to-all-start.3 = ((f32[32,16,128]{2,1,0:T(8,128)}), f32[32,16,128]{2,1,0:T(8,128)S(1)}, u32[]{:S(2)}, u32[]{:S(2)}) async-start(f32[32,16,128]{2,1,0:T(8,128)} %broadcast_in_dim.8), calls=%async_computation.3 | async-start | bytes 524288 | tf_op jit(solution)/shard_map/sums_all/all_to_all | solution.py:361
  132.4 1.0 copy-done.2
  133.4 5.5 %input_grad.1 = bf16[128,4096]{1,0:T(8,128)(2,1)} custom-call(f32[128,4096]{1,0:T(8,128)} %own_rows.1.refs_0_, bf16[128,4096]{1,0:T(8,128)(2,1)} %copy-done.2, bf16[128,256]{1,0:T(8,128)(2,1)} %refs_2_.3, bf16[256,256]{1,0:T(8,128)(2,1)} %constant.17.refs_4_.refs_2_.refs_3_, bf16[256,256]{1,0:T(8,128)(2,1)} %constant.20.refs_7_.refs_4_, ...), custom_call_target="tpu_custom_call" | custom-call | flops 2147483648 | bytes 4194304 | tf_op jit(solution)/shard_map/input_grad/pallas_call | solution.py:349
  138.9 4.8 %all-to-all-done.3.refs_0_ = f32[32,16,128]{2,1,0:T(8,128)S(1)} async-done(((f32[32,16,128]{2,1,0:T(8,128)}), f32[32,16,128]{2,1,0:T(8,128)S(1)}, u32[]{:S(2)}, u32[]{:S(2)}) %all-to-all-start.3) | async-done | bytes 262176 | tf_op jit(solution)/shard_map/sums_all/all_to_all | solution.py:361
  143.7 0.8 finish.1
  (8 shorter events, 0.1 us)
Async XLA Ops:
  0.6 17.0 %collective-permute-start = (bf16[128,4096]{1,0:T(8,128)(2,1)}, bf16[128,4096]{1,0:T(8,128)(2,1)S(1)}, u32[]{:S(2)}, u32[]{:S(2)}) collective-permute-start(bf16[128,4096]{1,0:T(8,128)(2,1)} %bitcast.10), channel_id=1, source_target_pairs={{0,1},{1,2},{2,3},{3,4},{4,5},{5,6},{6,7},{7,8},{8,9},{9,10},{10,1... | collective-permute-start | bytes 3145736 | tf_op jit(solution)/shard_map/halo/ppermute | solution.py:278
  9.3 59.3 %all-to-all-start = ((bf16[32,8,4224]{2,1,0:T(8,128)(2,1)}), bf16[32,8,4224]{2,1,0:T(8,128)(2,1)}, u32[]{:S(2)}, u32[]{:S(2)}) async-start(bf16[32,8,4224]{2,1,0:T(8,128)(2,1)} %bitcast.6), calls=%async_computation | async-start | bytes 4325376 | tf_op jit(solution)/shard_map/route/all_to_all | solution.py:273
  17.6 1.0 copy-start.3
  25.8 26.7 %collective-permute-start.1 = (bf16[2,4096]{1,0:T(2,128)(2,1)S(1)}, bf16[2,4096]{1,0:T(2,128)(2,1)S(1)}, u32[]{:S(2)}, u32[]{:S(2)}) collective-permute-start(bf16[2,4096]{1,0:T(2,128)(2,1)S(1)} %slice.17), channel_id=1, source_target_pairs={{0,1},{1,2},{2,3},{3,4},{4,5},{5,6},{6,7},{7,8},{8,9},{9,10},{10,1... | collective-permute-start | bytes 49160 | tf_op jit(solution)/shard_map/tail/ppermute | solution.py:301
  52.5 16.0 %copy-start = (bf16[2,4096]{1,0:T(2,128)(2,1)}, bf16[2,4096]{1,0:T(2,128)(2,1)S(1)}, u32[]{:S(2)}) copy-start(bf16[2,4096]{1,0:T(2,128)(2,1)S(1)} %collective-permute-done.1.refs_5_) | copy-start | bytes 49156
  93.0 32.2 %all-to-all-start.2 = ((f32[16,16,128]{2,1,0:T(8,128)}), f32[16,16,128]{2,1,0:T(8,128)S(1)}, u32[]{:S(2)}, u32[]{:S(2)}) async-start(f32[16,16,128]{2,1,0:T(8,128)} %broadcast_in_dim.7), calls=%async_computation.2 | async-start | bytes 262144 | tf_op jit(solution)/shard_map/sums_dp/all_to_all | solution.py:347
  109.6 5.5 %copy-start.1 = (bf16[128,4096]{1,0:T(8,128)(2,1)S(1)}, bf16[128,4096]{1,0:T(8,128)(2,1)}, u32[]{:S(2)}) copy-start(bf16[128,4096]{1,0:T(8,128)(2,1)} %get-tuple-element.19.refs_0_) | copy-start | bytes 3145732
  115.0 17.3 %collective-permute-start.2 = (bf16[128,4096]{1,0:T(8,128)(2,1)S(1)}, bf16[128,4096]{1,0:T(8,128)(2,1)S(1)}, u32[]{:S(2)}, u32[]{:S(2)}) collective-permute-start(bf16[128,4096]{1,0:T(8,128)(2,1)S(1)} %copy-done.1), channel_id=1, source_target_pairs={{1,0},{2,1},{3,2},{4,3},{5,4},{6,5},{7,6},{8,7},{9,8},{10,9},{11,1... | collective-permute-start | bytes 3145736 | tf_op jit(solution)/shard_map/later/ppermute | solution.py:342
  125.9 17.7 %all-to-all-start.3 = ((f32[32,16,128]{2,1,0:T(8,128)}), f32[32,16,128]{2,1,0:T(8,128)S(1)}, u32[]{:S(2)}, u32[]{:S(2)}) async-start(f32[32,16,128]{2,1,0:T(8,128)} %broadcast_in_dim.8), calls=%async_computation.3 | async-start | bytes 524288 | tf_op jit(solution)/shard_map/sums_all/all_to_all | solution.py:361
  132.4 1.0 copy-start.2

commit v5 on v4

--- a/solution.py
+++ b/solution.py
@@ -137,7 +137,7 @@
     spec_ref,
 ):
     spec = forward(ft_ref[...], jnp.concatenate([prev_ref[...], own_ref[...]], axis=0))
-    spec_ref[...] = spec
+    spec_ref[...] = spec.astype(jnp.bfloat16)
     wave = filter_spec(taps_ref[...], fn_ref[...], per_group, own_ref.shape[1])
     sr, si = halved(spec)
     wr, wi = halved(wave)
@@ -177,13 +177,12 @@
     terms.append(jnp.zeros((8 - len(moved), tile), jnp.float32))
     short_terms = jnp.concatenate(terms, axis=0)
     gr, gi = halved(narrow(fn_ref[...], hgrad))
-    pr, pi = halved(spec_ref[...])
+    pr, pi = halved(spec_ref[...].astype(jnp.float32))
     cross = jnp.concatenate([gr * pr + gi * pi, gi * pr - gr * pi], axis=0)
     first = lax.broadcasted_iota(jnp.int32, (tile, groups), 1) * per_group
     channel = lax.broadcasted_iota(jnp.int32, (tile, groups), 0)
     member = ((channel >= first) & (channel < first + per_group)).astype(jnp.bfloat16)
-    top, rest = split(cross)
-    grouped = forward(jnp.concatenate([top, rest], axis=0), member)
+    grouped = mm(cross.astype(jnp.bfloat16), member)
     lagged = backward(ct_ref[...], grouped).T
     for part in range(tile // LANES):
         sums_ref[part, :8] = lagged[8 * part : 8 * part + 8]
@@ -291,7 +290,7 @@
             out_specs=[columns(rows), columns(2 * rows)],
             out_shape=[
                 jax.ShapeDtypeStruct((rows, channels), f32),
-                jax.ShapeDtypeStruct((2 * rows, channels), f32),
+                jax.ShapeDtypeStruct((2 * rows, channels), bf16),
             ],
             compiler_params=params(60),
             cost_estimate=cost(10**14, 12 * MIB),

time: 145 us -> 144 us (level)
  transfers between devices with their start and end apart: 6 -> 6, of which waited for: 5 -> 5; matrix products, arithmetic and copies ran while one was open for 1% -> 1% of each run, Pallas kernels for 15% -> 14%
where the time goes in v5:
time: 144 us
  waiting for transfers between devices  52 us (36%)
  starting transfers between devices  42.2 us (29%)
  Pallas kernels  28.6 us (20%)
  blocking collectives  15.9 us (11%)
  local copies, waits for them, and re-layouts  4.2 us (3%)
    ppermute x1, waiting for transfers between devices, body(): tail = lax.ppermute(ending[rows - short_count + 1:], 'seq', onward)  22.7 us
    all_to_all x1, starting transfers between devices, body(): mine = jnp.sum(lax.all_to_all(spread, 'dp', 0, 0, tiled=True), axis=0)  16.6 us
    all_to_all x1, waiting for transfers between devices, body(): lax.all_to_all(send.reshape(shards, capacity, width), 'seq', split_axis=0...  16 us
    all_to_all x1, blocking collectives, body(): mine = jnp.sum(lax.all_to_all(sums, 'seq', 0, 0, tiled=True), axis=0)  15.9 us
    all_to_all x1, waiting for transfers between devices, body(): mine = jnp.sum(lax.all_to_all(spread, 'dp', 0, 0, tiled=True), axis=0)  7.9 us
    all_to_all x1, starting transfers between devices, body(): lax.all_to_all(send.reshape(shards, capacity, width), 'seq', split_axis=0...  7.7 us
    pallas_call x1, Pallas kernels, body(): pl.pallas_call(lambda *refs: grad_kernel(per_group, *refs), grid=(steps,)...  7.07 us
    all_to_all x1, starting transfers between devices, body(): total = lax.all_to_all(spread, 'seq', 0, 0, tiled=True)  6.45 us
  transfers between devices with their start and end apart: 6, of which 5 were waited for; matrix products, arithmetic and copies ran while one was open for 1% of the time, Pallas kernels for 14%

profile of v5, /device:TPU:1, one launch (start us, length us, event | category | flops | bytes accessed | tf_op | source)
XLA Modules:
  0.0 143.6 jit_solution(12519508000438513054)
XLA Ops:
  0.6 4.9 %collective-permute-start = (bf16[128,4096]{1,0:T(8,128)(2,1)}, bf16[128,4096]{1,0:T(8,128)(2,1)S(1)}, u32[]{:S(2)}, u32[]{:S(2)}) collective-permute-start(bf16[128,4096]{1,0:T(8,128)(2,1)} %bitcast.10), channel_id=1, source_target_pairs={{0,1},{1,2},{2,3},{3,4},{4,5},{5,6},{6,7},{7,8},{8,9},{9,10},{10,1... | collective-permute-start | bytes 3145736 | tf_op jit(solution)/shard_map/halo/ppermute | solution.py:277
  5.6 3.7 %pack.1 = bf16[256,4224]{1,0:T(8,128)(2,1)} custom-call(s32[1,128]{1,0:T(1,128)} %refs_0_.1, bf16[128,4096]{1,0:T(8,128)(2,1)} %bitcast.9), custom_call_target="tpu_custom_call" | custom-call | flops 276824064 | bytes 4194304 | tf_op jit(solution)/shard_map/pack/pallas_call | solution.py:254
  9.3 7.7 %all-to-all-start = ((bf16[32,8,4224]{2,1,0:T(8,128)(2,1)}), bf16[32,8,4224]{2,1,0:T(8,128)(2,1)}, u32[]{:S(2)}, u32[]{:S(2)}) async-start(bf16[32,8,4224]{2,1,0:T(8,128)(2,1)} %bitcast.6), calls=%async_computation | async-start | bytes 4325376 | tf_op jit(solution)/shard_map/route/all_to_all | solution.py:272
  17.0 0.6 collective-permute-done.refs_1_
  17.6 1.0 copy-done.3
  18.6 6.1 %early.1 = (f32[128,4096]{1,0:T(8,128)}, bf16[256,4096]{1,0:T(8,128)(2,1)}) custom-call(bf16[128,4096]{1,0:T(8,128)(2,1)} %bitcast.11, bf16[128,4096]{1,0:T(8,128)(2,1)} %copy-done.3, bf16[128,256]{1,0:T(8,128)(2,1)} %refs_2_.3, bf16[512,256]{1,0:T(8,128)(2,1)} %constant.8.clone.refs_3_, bf16[256,256]{1,0:T(8,128)(2,1)} %constant.17.refs_4_.refs_2_.refs_3_, ...), custom_call_target="tpu_custom_call" | custom-call | flops 100000000376832 | bytes 12582912 | tf_op jit(solution)/shard_map/early/pallas_call | solution.py:279
  24.7 0.9 slice.17
  25.6 4.3 %collective-permute-start.1 = (bf16[2,4096]{1,0:T(2,128)(2,1)S(1)}, bf16[2,4096]{1,0:T(2,128)(2,1)S(1)}, u32[]{:S(2)}, u32[]{:S(2)}) collective-permute-start(bf16[2,4096]{1,0:T(2,128)(2,1)S(1)} %slice.17), channel_id=1, source_target_pairs={{0,1},{1,2},{2,3},{3,4},{4,5},{5,6},{6,7},{7,8},{8,9},{9,10},{10,1... | collective-permute-start | bytes 49160 | tf_op jit(solution)/shard_map/tail/ppermute | solution.py:300
  29.8 22.7 %collective-permute-done.1.refs_5_ = bf16[2,4096]{1,0:T(2,128)(2,1)S(1)} collective-permute-done((bf16[2,4096]{1,0:T(2,128)(2,1)S(1)}, bf16[2,4096]{1,0:T(2,128)(2,1)S(1)}, u32[]{:S(2)}, u32[]{:S(2)}) %collective-permute-start.1) | collective-permute-done | bytes 16416 | tf_op jit(solution)/shard_map/tail/ppermute | solution.py:300
  52.5 16.0 %all-to-all-done = bf16[32,8,4224]{2,1,0:T(8,128)(2,1)} async-done(((bf16[32,8,4224]{2,1,0:T(8,128)(2,1)}), bf16[32,8,4224]{2,1,0:T(8,128)(2,1)}, u32[]{:S(2)}, u32[]{:S(2)}) %all-to-all-start) | async-done | bytes 2162720 | tf_op jit(solution)/shard_map/route/all_to_all | solution.py:272
  68.6 7.1 %grads.1 = (bf16[128,4096]{1,0:T(8,128)(2,1)}, f32[32,16,128]{2,1,0:T(8,128)}) custom-call(bf16[256,4224]{1,0:T(8,128)(2,1)} %bitcast.2.refs_0_.refs_1_, bf16[256,4224]{1,0:T(8,128)(2,1)} %bitcast.2.refs_0_.refs_1_, f32[128,4096]{1,0:T(8,128)} %get-tuple-element.14.refs_2_, bf16[256,4096]{1,0:T(8,128)(2,1)} %get-tuple-element.15.refs_3_, ...), custom_call_target="tpu_custom_call" | custom-call | flops 1342177280 | bytes 12582912 | tf_op jit(solution)/shard_map/grads/pallas_call | solution.py:302
  75.6 15.9 %all_to_all.20 = f32[32,16,128]{2,1,0:T(8,128)S(1)} all-to-all(f32[32,16,128]{2,1,0:T(8,128)} %get-tuple-element.20), channel_id=1, replica_groups=mesh['dp'=16,'seq'=32] {'seq'}, dimensions={0} | all-to-all | bytes 524288 | tf_op jit(solution)/shard_map/sums_seq/all_to_all | solution.py:328
  91.5 0.7 broadcast_in_dim.7
  92.2 16.6 %all-to-all-start.2 = ((f32[16,16,128]{2,1,0:T(8,128)}), f32[16,16,128]{2,1,0:T(8,128)S(1)}, u32[]{:S(2)}, u32[]{:S(2)}) async-start(f32[16,16,128]{2,1,0:T(8,128)} %broadcast_in_dim.7), calls=%async_computation.2 | async-start | bytes 262144 | tf_op jit(solution)/shard_map/sums_dp/all_to_all | solution.py:346
  108.8 0.0 copy-start.1
  108.8 5.4 %own_rows.1.refs_0_ = f32[128,4096]{1,0:T(8,128)} custom-call(bf16[128,4096]{1,0:T(8,128)(2,1)} %get-tuple-element.19.refs_0_, bf16[128,256]{1,0:T(8,128)(2,1)} %refs_2_.3, bf16[256,256]{1,0:T(8,128)(2,1)} %constant.17.refs_4_.refs_2_.refs_3_, bf16[256,256]{1,0:T(8,128)(2,1)} %constant.9.clone.refs_8_.refs_3_.refs_5_), custom_call_target="tpu_custom_call" | custom-call | flops 2147483648 | bytes 3145728 | tf_op jit(solution)/shard_map/own_rows/pallas_call | solution.py:330
  114.3 2.2 %collective-permute-start.2 = (bf16[128,4096]{1,0:T(8,128)(2,1)S(1)}, bf16[128,4096]{1,0:T(8,128)(2,1)S(1)}, u32[]{:S(2)}, u32[]{:S(2)}) collective-permute-start(bf16[128,4096]{1,0:T(8,128)(2,1)S(1)} %copy-done.1), channel_id=1, source_target_pairs={{1,0},{2,1},{3,2},{4,3},{5,4},{6,5},{7,6},{8,7},{9,8},{10,9},{11,1... | collective-permute-start | bytes 3145736 | tf_op jit(solution)/shard_map/later/ppermute | solution.py:341
  116.5 7.9 %all-to-all-done.2 = f32[16,16,128]{2,1,0:T(8,128)S(1)} async-done(((f32[16,16,128]{2,1,0:T(8,128)}), f32[16,16,128]{2,1,0:T(8,128)S(1)}, u32[]{:S(2)}, u32[]{:S(2)}) %all-to-all-start.2) | async-done | bytes 131104 | tf_op jit(solution)/shard_map/sums_dp/all_to_all | solution.py:346
  124.4 0.7 broadcast_in_dim.8
  125.1 6.4 %all-to-all-start.3 = ((f32[32,16,128]{2,1,0:T(8,128)}), f32[32,16,128]{2,1,0:T(8,128)S(1)}, u32[]{:S(2)}, u32[]{:S(2)}) async-start(f32[32,16,128]{2,1,0:T(8,128)} %broadcast_in_dim.8), calls=%async_computation.3 | async-start | bytes 524288 | tf_op jit(solution)/shard_map/sums_all/all_to_all | solution.py:360
  131.6 1.0 copy-done.2
  132.6 5.5 %input_grad.1 = bf16[128,4096]{1,0:T(8,128)(2,1)} custom-call(f32[128,4096]{1,0:T(8,128)} %own_rows.1.refs_0_, bf16[128,4096]{1,0:T(8,128)(2,1)} %copy-done.2, bf16[128,256]{1,0:T(8,128)(2,1)} %refs_2_.3, bf16[256,256]{1,0:T(8,128)(2,1)} %constant.17.refs_4_.refs_2_.refs_3_, bf16[256,256]{1,0:T(8,128)(2,1)} %constant.20.refs_7_.refs_4_, ...), custom_call_target="tpu_custom_call" | custom-call | flops 2147483648 | bytes 4194304 | tf_op jit(solution)/shard_map/input_grad/pallas_call | solution.py:348
  138.1 4.8 %all-to-all-done.3.refs_0_ = f32[32,16,128]{2,1,0:T(8,128)S(1)} async-done(((f32[32,16,128]{2,1,0:T(8,128)}), f32[32,16,128]{2,1,0:T(8,128)S(1)}, u32[]{:S(2)}, u32[]{:S(2)}) %all-to-all-start.3) | async-done | bytes 262176 | tf_op jit(solution)/shard_map/sums_all/all_to_all | solution.py:360
  142.9 0.8 finish.1
  (8 shorter events, 0.1 us)
Async XLA Ops:
  0.6 17.0 %collective-permute-start = (bf16[128,4096]{1,0:T(8,128)(2,1)}, bf16[128,4096]{1,0:T(8,128)(2,1)S(1)}, u32[]{:S(2)}, u32[]{:S(2)}) collective-permute-start(bf16[128,4096]{1,0:T(8,128)(2,1)} %bitcast.10), channel_id=1, source_target_pairs={{0,1},{1,2},{2,3},{3,4},{4,5},{5,6},{6,7},{7,8},{8,9},{9,10},{10,1... | collective-permute-start | bytes 3145736 | tf_op jit(solution)/shard_map/halo/ppermute | solution.py:277
  9.3 59.3 %all-to-all-start = ((bf16[32,8,4224]{2,1,0:T(8,128)(2,1)}), bf16[32,8,4224]{2,1,0:T(8,128)(2,1)}, u32[]{:S(2)}, u32[]{:S(2)}) async-start(bf16[32,8,4224]{2,1,0:T(8,128)(2,1)} %bitcast.6), calls=%async_computation | async-start | bytes 4325376 | tf_op jit(solution)/shard_map/route/all_to_all | solution.py:272
  17.6 1.0 copy-start.3
  25.6 27.0 %collective-permute-start.1 = (bf16[2,4096]{1,0:T(2,128)(2,1)S(1)}, bf16[2,4096]{1,0:T(2,128)(2,1)S(1)}, u32[]{:S(2)}, u32[]{:S(2)}) collective-permute-start(bf16[2,4096]{1,0:T(2,128)(2,1)S(1)} %slice.17), channel_id=1, source_target_pairs={{0,1},{1,2},{2,3},{3,4},{4,5},{5,6},{6,7},{7,8},{8,9},{9,10},{10,1... | collective-permute-start | bytes 49160 | tf_op jit(solution)/shard_map/tail/ppermute | solution.py:300
  52.5 16.1 %copy-start = (bf16[2,4096]{1,0:T(2,128)(2,1)}, bf16[2,4096]{1,0:T(2,128)(2,1)S(1)}, u32[]{:S(2)}) copy-start(bf16[2,4096]{1,0:T(2,128)(2,1)S(1)} %collective-permute-done.1.refs_5_) | copy-start | bytes 49156
  92.2 32.2 %all-to-all-start.2 = ((f32[16,16,128]{2,1,0:T(8,128)}), f32[16,16,128]{2,1,0:T(8,128)S(1)}, u32[]{:S(2)}, u32[]{:S(2)}) async-start(f32[16,16,128]{2,1,0:T(8,128)} %broadcast_in_dim.7), calls=%async_computation.2 | async-start | bytes 262144 | tf_op jit(solution)/shard_map/sums_dp/all_to_all | solution.py:346
  108.8 5.5 %copy-start.1 = (bf16[128,4096]{1,0:T(8,128)(2,1)S(1)}, bf16[128,4096]{1,0:T(8,128)(2,1)}, u32[]{:S(2)}) copy-start(bf16[128,4096]{1,0:T(8,128)(2,1)} %get-tuple-element.19.refs_0_) | copy-start | bytes 3145732
  114.3 17.3 %collective-permute-start.2 = (bf16[128,4096]{1,0:T(8,128)(2,1)S(1)}, bf16[128,4096]{1,0:T(8,128)(2,1)S(1)}, u32[]{:S(2)}, u32[]{:S(2)}) collective-permute-start(bf16[128,4096]{1,0:T(8,128)(2,1)S(1)} %copy-done.1), channel_id=1, source_target_pairs={{1,0},{2,1},{3,2},{4,3},{5,4},{6,5},{7,6},{8,7},{9,8},{10,9},{11,1... | collective-permute-start | bytes 3145736 | tf_op jit(solution)/shard_map/later/ppermute | solution.py:341
  125.1 17.7 %all-to-all-start.3 = ((f32[32,16,128]{2,1,0:T(8,128)}), f32[32,16,128]{2,1,0:T(8,128)S(1)}, u32[]{:S(2)}, u32[]{:S(2)}) async-start(f32[32,16,128]{2,1,0:T(8,128)} %broadcast_in_dim.8), calls=%async_computation.3 | async-start | bytes 524288 | tf_op jit(solution)/shard_map/sums_all/all_to_all | solution.py:360
  131.6 1.0 copy-start.2

commit v6 on v5

--- a/solution.py
+++ b/solution.py
@@ -185,8 +185,9 @@
     grouped = mm(cross.astype(jnp.bfloat16), member)
     lagged = backward(ct_ref[...], grouped).T
     for part in range(tile // LANES):
-        sums_ref[part, :8] = lagged[8 * part : 8 * part + 8]
-        sums_ref[part, 8:] = short_terms[:, part * LANES : (part + 1) * LANES]
+        terms = short_terms[:, part * LANES : (part + 1) * LANES]
+        both = jnp.concatenate([lagged[8 * part : 8 * part + 8], terms], axis=0)
+        sums_ref[part] = both.astype(jnp.bfloat16)
 
 
 def own_kernel(per_group, own_ref, taps_ref, fn_ref, it_ref, part_ref):
@@ -319,13 +320,14 @@
             ],
             out_shape=[
                 jax.ShapeDtypeStruct((rows, channels), bf16),
-                jax.ShapeDtypeStruct((channels // LANES, BLOCK_ROWS, LANES), f32),
+                jax.ShapeDtypeStruct((channels // LANES, BLOCK_ROWS, LANES), bf16),
             ],
             compiler_params=params(60),
             cost_estimate=cost(10 * rows * 2 * rows * channels, 12 * MIB),
         )(recv, recv, hidden, spec, query, tail, short_filter, upper, first)
     with jax.named_scope("sums_seq"):
-        mine = jnp.sum(lax.all_to_all(sums, "seq", 0, 0, tiled=True), axis=0)
+        shares = lax.all_to_all(sums, "seq", 0, 0, tiled=True)
+        mine = jnp.sum(shares.astype(f32), axis=0)
     with jax.named_scope("own_rows"):
         part = pl.pallas_call(
             lambda *refs: own_kernel(per_group, *refs),

time: 144 us -> 142 us (0.986)
  blocking collectives: 15.9 us -> 13.3 us
    all_to_all x1, blocking collectives: 15.9 us -> 13.3 us  [body(): shares = lax.all_to_all(sums, 'seq', 0, 0, tiled=True)]
  transfers between devices with their start and end apart: 6 -> 6, of which waited for: 5 -> 5; matrix products, arithmetic and copies ran while one was open for 1% -> 1% of each run, Pallas kernels for 14% -> 15%
where the time goes in v6:
time: 142 us; the launch traced here: 141 us
  waiting for transfers between devices  51.3 us (36%)
  starting transfers between devices  42.9 us (30%)
  Pallas kernels  28.5 us (20%)
  blocking collectives  13.3 us (9%)
  local copies, waits for them, and re-layouts  4.2 us (3%)
    ppermute x1, waiting for transfers between devices, body(): tail = lax.ppermute(ending[rows - short_count + 1:], 'seq', onward)  22.7 us
    all_to_all x1, starting transfers between devices, body(): mine = jnp.sum(lax.all_to_all(spread, 'dp', 0, 0, tiled=True), axis=0)  16.6 us
    all_to_all x1, waiting for transfers between devices, body(): lax.all_to_all(send.reshape(shards, capacity, width), 'seq', split_axis=0...  16 us
    all_to_all x1, blocking collectives, body(): shares = lax.all_to_all(sums, 'seq', 0, 0, tiled=True)  13.3 us
    all_to_all x1, starting transfers between devices, body(): lax.all_to_all(send.reshape(shards, capacity, width), 'seq', split_axis=0...  7.7 us
    all_to_all x1, waiting for transfers between devices, body(): mine = jnp.sum(lax.all_to_all(spread, 'dp', 0, 0, tiled=True), axis=0)  7.22 us
    pallas_call x1, Pallas kernels, body(): pl.pallas_call(lambda *refs: grad_kernel(per_group, *refs), grid=(steps,)...  6.98 us
    all_to_all x1, starting transfers between devices, body(): total = lax.all_to_all(spread, 'seq', 0, 0, tiled=True)  6.85 us
  transfers between devices with their start and end apart: 6, of which 5 were waited for; matrix products, arithmetic and copies ran while one was open for 1% of the time, Pallas kernels for 15%

profile of v6, /device:TPU:1, one launch (start us, length us, event | category | flops | bytes accessed | tf_op | source)
XLA Modules:
  0.0 141.0 jit_solution(17275237316758646605)
XLA Ops:
  0.6 4.9 %collective-permute-start = (bf16[128,4096]{1,0:T(8,128)(2,1)}, bf16[128,4096]{1,0:T(8,128)(2,1)S(1)}, u32[]{:S(2)}, u32[]{:S(2)}) collective-permute-start(bf16[128,4096]{1,0:T(8,128)(2,1)} %bitcast.10), channel_id=1, source_target_pairs={{0,1},{1,2},{2,3},{3,4},{4,5},{5,6},{6,7},{7,8},{8,9},{9,10},{10,1... | collective-permute-start | bytes 3145736 | tf_op jit(solution)/shard_map/halo/ppermute | solution.py:278
  5.6 3.7 %pack.1 = bf16[256,4224]{1,0:T(8,128)(2,1)} custom-call(s32[1,128]{1,0:T(1,128)} %refs_0_.1, bf16[128,4096]{1,0:T(8,128)(2,1)} %bitcast.9), custom_call_target="tpu_custom_call" | custom-call | flops 276824064 | bytes 4194304 | tf_op jit(solution)/shard_map/pack/pallas_call | solution.py:255
  9.3 7.7 %all-to-all-start = ((bf16[32,8,4224]{2,1,0:T(8,128)(2,1)}), bf16[32,8,4224]{2,1,0:T(8,128)(2,1)}, u32[]{:S(2)}, u32[]{:S(2)}) async-start(bf16[32,8,4224]{2,1,0:T(8,128)(2,1)} %bitcast.6), calls=%async_computation | async-start | bytes 4325376 | tf_op jit(solution)/shard_map/route/all_to_all | solution.py:273
  17.0 0.6 collective-permute-done.refs_1_
  17.6 1.0 copy-done.3
  18.6 6.1 %early.1 = (f32[128,4096]{1,0:T(8,128)}, bf16[256,4096]{1,0:T(8,128)(2,1)}) custom-call(bf16[128,4096]{1,0:T(8,128)(2,1)} %bitcast.11, bf16[128,4096]{1,0:T(8,128)(2,1)} %copy-done.3, bf16[128,256]{1,0:T(8,128)(2,1)} %refs_2_.3, bf16[512,256]{1,0:T(8,128)(2,1)} %constant.8.clone.refs_3_, bf16[256,256]{1,0:T(8,128)(2,1)} %constant.17.refs_4_.refs_2_.refs_3_, ...), custom_call_target="tpu_custom_call" | custom-call | flops 100000000376832 | bytes 12582912 | tf_op jit(solution)/shard_map/early/pallas_call | solution.py:280
  24.7 0.9 slice.17
  25.6 4.3 %collective-permute-start.1 = (bf16[2,4096]{1,0:T(2,128)(2,1)S(1)}, bf16[2,4096]{1,0:T(2,128)(2,1)S(1)}, u32[]{:S(2)}, u32[]{:S(2)}) collective-permute-start(bf16[2,4096]{1,0:T(2,128)(2,1)S(1)} %slice.17), channel_id=1, source_target_pairs={{0,1},{1,2},{2,3},{3,4},{4,5},{5,6},{6,7},{7,8},{8,9},{9,10},{10,1... | collective-permute-start | bytes 49160 | tf_op jit(solution)/shard_map/tail/ppermute | solution.py:301
  29.8 22.7 %collective-permute-done.1.refs_5_ = bf16[2,4096]{1,0:T(2,128)(2,1)S(1)} collective-permute-done((bf16[2,4096]{1,0:T(2,128)(2,1)S(1)}, bf16[2,4096]{1,0:T(2,128)(2,1)S(1)}, u32[]{:S(2)}, u32[]{:S(2)}) %collective-permute-start.1) | collective-permute-done | bytes 16416 | tf_op jit(solution)/shard_map/tail/ppermute | solution.py:301
  52.5 16.0 %all-to-all-done = bf16[32,8,4224]{2,1,0:T(8,128)(2,1)} async-done(((bf16[32,8,4224]{2,1,0:T(8,128)(2,1)}), bf16[32,8,4224]{2,1,0:T(8,128)(2,1)}, u32[]{:S(2)}, u32[]{:S(2)}) %all-to-all-start) | async-done | bytes 2162720 | tf_op jit(solution)/shard_map/route/all_to_all | solution.py:273
  68.6 7.0 %grads.1 = (bf16[128,4096]{1,0:T(8,128)(2,1)}, bf16[32,16,128]{2,1,0:T(8,128)(2,1)}) custom-call(bf16[256,4224]{1,0:T(8,128)(2,1)} %bitcast.2.refs_0_.refs_1_, bf16[256,4224]{1,0:T(8,128)(2,1)} %bitcast.2.refs_0_.refs_1_, f32[128,4096]{1,0:T(8,128)} %get-tuple-element.14.refs_2_, bf16[256,4096]{1,0:T(8,128)(2,1)} %get-tuple-element.15.refs_3_, ...), custom_call_target="tpu_custom_call" | custom-call | flops 1342177280 | bytes 12582912 | tf_op jit(solution)/shard_map/grads/pallas_call | solution.py:303
  75.5 13.3 %all_to_all.20 = bf16[32,16,128]{2,1,0:T(8,128)(2,1)S(1)} all-to-all(bf16[32,16,128]{2,1,0:T(8,128)(2,1)} %get-tuple-element.20), channel_id=1, replica_groups=mesh['dp'=16,'seq'=32] {'seq'}, dimensions={0} | all-to-all | bytes 262144 | tf_op jit(solution)/shard_map/sums_seq/all_to_all | solution.py:329
  88.9 0.7 broadcast_in_dim.7
  89.5 16.6 %all-to-all-start.2 = ((f32[16,16,128]{2,1,0:T(8,128)}), f32[16,16,128]{2,1,0:T(8,128)S(1)}, u32[]{:S(2)}, u32[]{:S(2)}) async-start(f32[16,16,128]{2,1,0:T(8,128)} %broadcast_in_dim.7), calls=%async_computation.2 | async-start | bytes 262144 | tf_op jit(solution)/shard_map/sums_dp/all_to_all | solution.py:348
  106.1 0.0 copy-start.1
  106.2 5.4 %own_rows.1.refs_0_ = f32[128,4096]{1,0:T(8,128)} custom-call(bf16[128,4096]{1,0:T(8,128)(2,1)} %get-tuple-element.19.refs_0_, bf16[128,256]{1,0:T(8,128)(2,1)} %refs_2_.3, bf16[256,256]{1,0:T(8,128)(2,1)} %constant.17.refs_4_.refs_2_.refs_3_, bf16[256,256]{1,0:T(8,128)(2,1)} %constant.9.clone.refs_8_.refs_3_.refs_5_), custom_call_target="tpu_custom_call" | custom-call | flops 2147483648 | bytes 3145728 | tf_op jit(solution)/shard_map/own_rows/pallas_call | solution.py:332
  111.6 2.6 %collective-permute-start.2 = (bf16[128,4096]{1,0:T(8,128)(2,1)S(1)}, bf16[128,4096]{1,0:T(8,128)(2,1)S(1)}, u32[]{:S(2)}, u32[]{:S(2)}) collective-permute-start(bf16[128,4096]{1,0:T(8,128)(2,1)S(1)} %copy-done.1), channel_id=1, source_target_pairs={{1,0},{2,1},{3,2},{4,3},{5,4},{6,5},{7,6},{8,7},{9,8},{10,9},{11,1... | collective-permute-start | bytes 3145736 | tf_op jit(solution)/shard_map/later/ppermute | solution.py:343
  114.2 7.2 %all-to-all-done.2 = f32[16,16,128]{2,1,0:T(8,128)S(1)} async-done(((f32[16,16,128]{2,1,0:T(8,128)}), f32[16,16,128]{2,1,0:T(8,128)S(1)}, u32[]{:S(2)}, u32[]{:S(2)}) %all-to-all-start.2) | async-done | bytes 131104 | tf_op jit(solution)/shard_map/sums_dp/all_to_all | solution.py:348
  121.4 0.7 broadcast_in_dim.8
  122.1 6.9 %all-to-all-start.3 = ((f32[32,16,128]{2,1,0:T(8,128)}), f32[32,16,128]{2,1,0:T(8,128)S(1)}, u32[]{:S(2)}, u32[]{:S(2)}) async-start(f32[32,16,128]{2,1,0:T(8,128)} %broadcast_in_dim.8), calls=%async_computation.3 | async-start | bytes 524288 | tf_op jit(solution)/shard_map/sums_all/all_to_all | solution.py:362
  129.0 1.0 copy-done.2
  130.0 5.5 %input_grad.1 = bf16[128,4096]{1,0:T(8,128)(2,1)} custom-call(f32[128,4096]{1,0:T(8,128)} %own_rows.1.refs_0_, bf16[128,4096]{1,0:T(8,128)(2,1)} %copy-done.2, bf16[128,256]{1,0:T(8,128)(2,1)} %refs_2_.3, bf16[256,256]{1,0:T(8,128)(2,1)} %constant.17.refs_4_.refs_2_.refs_3_, bf16[256,256]{1,0:T(8,128)(2,1)} %constant.20.refs_7_.refs_4_, ...), custom_call_target="tpu_custom_call" | custom-call | flops 2147483648 | bytes 4194304 | tf_op jit(solution)/shard_map/input_grad/pallas_call | solution.py:350
  135.5 4.8 %all-to-all-done.3.refs_0_ = f32[32,16,128]{2,1,0:T(8,128)S(1)} async-done(((f32[32,16,128]{2,1,0:T(8,128)}), f32[32,16,128]{2,1,0:T(8,128)S(1)}, u32[]{:S(2)}, u32[]{:S(2)}) %all-to-all-start.3) | async-done | bytes 262176 | tf_op jit(solution)/shard_map/sums_all/all_to_all | solution.py:362
  140.3 0.8 finish.1
  (8 shorter events, 0.1 us)
Async XLA Ops:
  0.6 17.0 %collective-permute-start = (bf16[128,4096]{1,0:T(8,128)(2,1)}, bf16[128,4096]{1,0:T(8,128)(2,1)S(1)}, u32[]{:S(2)}, u32[]{:S(2)}) collective-permute-start(bf16[128,4096]{1,0:T(8,128)(2,1)} %bitcast.10), channel_id=1, source_target_pairs={{0,1},{1,2},{2,3},{3,4},{4,5},{5,6},{6,7},{7,8},{8,9},{9,10},{10,1... | collective-permute-start | bytes 3145736 | tf_op jit(solution)/shard_map/halo/ppermute | solution.py:278
  9.3 59.3 %all-to-all-start = ((bf16[32,8,4224]{2,1,0:T(8,128)(2,1)}), bf16[32,8,4224]{2,1,0:T(8,128)(2,1)}, u32[]{:S(2)}, u32[]{:S(2)}) async-start(bf16[32,8,4224]{2,1,0:T(8,128)(2,1)} %bitcast.6), calls=%async_computation | async-start | bytes 4325376 | tf_op jit(solution)/shard_map/route/all_to_all | solution.py:273
  17.6 1.0 copy-start.3
  25.6 27.0 %collective-permute-start.1 = (bf16[2,4096]{1,0:T(2,128)(2,1)S(1)}, bf16[2,4096]{1,0:T(2,128)(2,1)S(1)}, u32[]{:S(2)}, u32[]{:S(2)}) collective-permute-start(bf16[2,4096]{1,0:T(2,128)(2,1)S(1)} %slice.17), channel_id=1, source_target_pairs={{0,1},{1,2},{2,3},{3,4},{4,5},{5,6},{6,7},{7,8},{8,9},{9,10},{10,1... | collective-permute-start | bytes 49160 | tf_op jit(solution)/shard_map/tail/ppermute | solution.py:301
  52.5 16.1 %copy-start = (bf16[2,4096]{1,0:T(2,128)(2,1)}, bf16[2,4096]{1,0:T(2,128)(2,1)S(1)}, u32[]{:S(2)}) copy-start(bf16[2,4096]{1,0:T(2,128)(2,1)S(1)} %collective-permute-done.1.refs_5_) | copy-start | bytes 49156
  89.5 31.9 %all-to-all-start.2 = ((f32[16,16,128]{2,1,0:T(8,128)}), f32[16,16,128]{2,1,0:T(8,128)S(1)}, u32[]{:S(2)}, u32[]{:S(2)}) async-start(f32[16,16,128]{2,1,0:T(8,128)} %broadcast_in_dim.7), calls=%async_computation.2 | async-start | bytes 262144 | tf_op jit(solution)/shard_map/sums_dp/all_to_all | solution.py:348
  106.1 5.5 %copy-start.1 = (bf16[128,4096]{1,0:T(8,128)(2,1)S(1)}, bf16[128,4096]{1,0:T(8,128)(2,1)}, u32[]{:S(2)}) copy-start(bf16[128,4096]{1,0:T(8,128)(2,1)} %get-tuple-element.19.refs_0_) | copy-start | bytes 3145732
  111.6 17.4 %collective-permute-start.2 = (bf16[128,4096]{1,0:T(8,128)(2,1)S(1)}, bf16[128,4096]{1,0:T(8,128)(2,1)S(1)}, u32[]{:S(2)}, u32[]{:S(2)}) collective-permute-start(bf16[128,4096]{1,0:T(8,128)(2,1)S(1)} %copy-done.1), channel_id=1, source_target_pairs={{1,0},{2,1},{3,2},{4,3},{5,4},{6,5},{7,6},{8,7},{9,8},{10,9},{11,1... | collective-permute-start | bytes 3145736 | tf_op jit(solution)/shard_map/later/ppermute | solution.py:343
  122.1 18.1 %all-to-all-start.3 = ((f32[32,16,128]{2,1,0:T(8,128)}), f32[32,16,128]{2,1,0:T(8,128)S(1)}, u32[]{:S(2)}, u32[]{:S(2)}) async-start(f32[32,16,128]{2,1,0:T(8,128)} %broadcast_in_dim.8), calls=%async_computation.3 | async-start | bytes 524288 | tf_op jit(solution)/shard_map/sums_all/all_to_all | solution.py:362
  129.0 1.0 copy-start.2
